TPU v7x, 256 devices: a whole 4x4x8 slice. The times are simulated.
256 devices in a mesh: rows: 16 (over z_hi, y, core), tp: 16 (over x, z_lo).
Axes of the slice: x: 4, y: 4, z: 8 (z_hi: 2, z_lo: 4; z = z_hi * 4 + z_lo), core: 2. Of those that a mesh axis runs over, the one named last changes fastest.
Arguments:
- teacher_hidden: bfloat16 [12288, 8192], P('rows', 'tp'), may hold values from -8 to 8
- norm_gain: float32 [8192], replicated, may hold values from 0.25 to 1.75
- head_weight: bfloat16 [8192, 16384], P('rows', 'tp'), may hold values from -0.19997864 to 0.19997864
- student_logits: bfloat16 [12288, 16384], P('rows', 'tp'), may hold values from -300 to 300
- row_lengths: int32 [3072], P('rows'), may hold values from 1 to 4
Outputs:
- logit_grad: bfloat16 [12288, 16384], P('rows', 'tp')
- loss: float32 [], replicated
All inputs are finite; a program needn't handle non-finite values.
Results may differ from a plain program's by a relative error of at most 0.0049.
Values may be sent and summed in bfloat16 or wider, within the bound.
No kernel may reach another device: no remote copies, remote signals or barrier semaphores. Data moves between devices by JAX's collectives and lax.ppermute only.
A program may use at most 128 MiB of HBM per device.

v0:
```python
import jax
import jax.numpy as jnp
from jax import lax
from jax.sharding import PartitionSpec as P

V = 2048
CB = 8
STEPS = 4


very_low = -1e30


def merged(shard, axis, combine):
    everything = jax.tree.map(lambda part: lax.all_gather(part, axis), shard)
    first = jax.tree.map(lambda part: part[0], everything)

    def step(k, so_far):
        return combine(so_far, jax.tree.map(lambda part: part[k], everything))

    return lax.fori_loop(1, lax.axis_size(axis), step, first)


def combine_pair(first, second):
    peak = jnp.maximum(first[0], second[0])
    total = first[1] * jnp.exp(first[0] - peak) + second[1] * jnp.exp(second[0] - peak)
    return (peak, total)


def combine_stats(first, second):
    teach = combine_pair((first[0], first[1]), (second[0], second[1]))
    stud = combine_pair((first[2], first[3]), (second[2], second[3]))
    return (teach[0], teach[1], stud[0], stud[1])


def spread_cols(values, member):
    return jnp.dot(values, member.T, precision=lax.Precision.HIGHEST)


def local_stats(logits, member, inside):
    peak = jnp.max(jnp.where(inside, logits[:, :, None], very_low), axis=1)
    total = jnp.dot(
        jnp.exp(logits - spread_cols(peak, member)), member, precision=lax.Precision.HIGHEST
    )
    return (peak, total)


def body(teacher_hidden, norm_gain, head_weight, student_logits, row_lengths):
    local_cols = head_weight.shape[1]
    tok_count = teacher_hidden.shape[0]
    first_col = lax.axis_index("tp") * local_cols
    book_of = (first_col + jnp.arange(local_cols, dtype=jnp.int32)) // V
    member = (book_of[:, None] == jnp.arange(CB, dtype=jnp.int32)[None, :]).astype(jnp.float32)
    inside = member[None, :, :] > 0.5
    student = student_logits.astype(jnp.float32)
    stud_peak, stud_total = local_stats(student, member, inside)
    gathered = lax.all_gather(teacher_hidden, "tp", axis=1, tiled=True)
    wide = gathered.astype(jnp.float32)
    scale = lax.rsqrt(jnp.mean(wide * wide, axis=-1) + 1e-05)
    normed = (wide * norm_gain[None, :]).astype(jnp.bfloat16)
    teacher = (
        jnp.dot(
            normed,
            lax.all_gather(head_weight, "rows", axis=0, tiled=True),
            preferred_element_type=jnp.float32,
        )
        * scale[:, None]
    )
    teach_peak, teach_total = local_stats(teacher, member, inside)
    teach_peak, teach_total, stud_peak, stud_total = merged(
        (teach_peak, teach_total, stud_peak, stud_total), "tp", combine_stats
    )
    teacher_logp = teacher - spread_cols(teach_peak + jnp.log(teach_total), member)
    student_logp = student - spread_cols(stud_peak + jnp.log(stud_total), member)
    prob = jnp.exp(student_logp)
    differ = student_logp - teacher_logp
    partial_value = jnp.dot(prob * differ, member, precision=lax.Precision.HIGHEST)
    divergence = lax.psum(partial_value, "tp")
    steps_of = jnp.arange(tok_count, dtype=jnp.int32) % STEPS
    live = (steps_of < jnp.repeat(row_lengths, STEPS)).astype(jnp.float32)
    grad = V * live[:, None] * prob * (differ - spread_cols(divergence, member))
    local_loss = jnp.sum(live[:, None] * divergence)
    local_len = jnp.sum(row_lengths.astype(jnp.float32))
    loss_sum, len_sum = lax.psum((local_loss, local_len), "rows")
    return (grad.astype(jnp.bfloat16), loss_sum / (CB * len_sum))


def solution(mesh):
    in_specs = (P("rows", "tp"), P(), P("rows", "tp"), P("rows", "tp"), P("rows"))
    out_specs = (P("rows", "tp"), P())
    return jax.shard_map(body, mesh=mesh, in_specs=in_specs, out_specs=out_specs, check_vma=False)
```

profile of v0, /device:TPU:2, one launch (start us, length us, event | category | flops | bytes accessed | tf_op | source)
XLA Modules:
  0.0 1006.4 jit_solution(2641041899739190471)
XLA Ops:
  7.2 0.0 all-gather.7.cloned.1.call-start
  7.2 0.7 all-gather.7.cloned.1.call-update
  7.9 0.0 copy-start.5
  7.9 0.0 all-gather.9.cloned.1.call-start
  8.0 0.7 all-gather.9.cloned.1.call-update
  8.7 0.8 broadcast_in_dim.41
  9.4 0.1 reshape.78
  9.5 1.8 convert_element_type.30
  11.3 0.0 copy-done.5
  11.4 0.7 convert_reduce_fusion
  12.1 0.0 copy-start.6
  12.1 270.2 %all-gather.7.cloned.1.call-done = bf16[768,8192]{1,0:T(8,128)(2,1)} async-done(((bf16[768,512]{1,0:T(8,128)(2,1)}), bf16[768,8192]{1,0:T(8,128)(2,1)}) %all-gather.7.cloned.1.call-update) | async-done | bytes 12582928 | tf_op jit(solution)/shard_map/all_gather | solution.py:57
  282.3 7.1 fusion.5
  289.4 171.2 %all-gather.9.cloned.1.call-done = bf16[8192,1024]{1,0:T(8,128)(2,1)} async-done(((bf16[512,1024]{1,0:T(8,128)(2,1)}), bf16[8192,1024]{1,0:T(8,128)(2,1)}) %all-gather.9.cloned.1.call-update) | async-done | bytes 16777232 | tf_op jit(solution)/shard_map/all_gather | solution.py:64
  460.6 0.0 copy-done.6
  460.6 18.8 %fusion.18 = f32[768,1024]{1,0:T(8,128)S(1)} fusion(bf16[8192,1024]{1,0:T(8,128)(2,1)} %all-gather.9.cloned.1.call-done, bf16[768,8192]{1,0:T(8,128)(2,1)} %all-gather.7.cloned.1.call-done, f32[8192]{0:T(1024)S(1)} %copy-done.6, f32[768]{0:T(1024)S(1)} %add_rsqrt_fusion), kind=kOutput, calls=%fused_computation.29 | convolution fusion | flops 12904562688 | bytes 32541696 | tf_op jit(solution)/shard_map/dot_general | solution.py:62
  479.4 0.0 copy-start
  479.4 8.6 select_reduce_fusion
  488.0 1.4 fusion.23
  489.4 141.4 %all-gather = f32[12288,8]{1,0:T(8,128)S(1)} all-gather(f32[768,8]{1,0:T(8,128)S(1)} %get-tuple-element.239), channel_id=2, replica_groups=mesh['rows'=16,'tp'=16] {'tp'}, dimensions={0}, use_global_device_ids=true | all-gather | bytes 417792 | tf_op jit(solution)/shard_map/all_gather | solution.py:15
  630.8 0.0 copy-start.3
  630.8 1.4 fusion.22
  632.2 0.0 copy-start.4
  632.2 142.2 %all-gather.2 = f32[12288,8]{1,0:T(8,128)} all-gather(f32[768,8]{1,0:T(8,128)S(1)} %get-tuple-element.238), channel_id=4, replica_groups=mesh['rows'=16,'tp'=16] {'tp'}, dimensions={0}, use_global_device_ids=true | all-gather | bytes 417792 | tf_op jit(solution)/shard_map/all_gather | solution.py:15
  774.3 0.0 copy-done.4
  774.4 1.9 fusion.11
  776.3 35.9 %all-gather.3 = f32[12288,8]{0,1:T(8,128)S(1)} all-gather(f32[768,8]{0,1:T(8,128)S(1)} %fusion.11), channel_id=5, replica_groups=mesh['rows'=16,'tp'=16] {'tp'}, dimensions={0}, use_global_device_ids=true | all-gather | bytes 417792 | tf_op jit(solution)/shard_map/all_gather | solution.py:15
  812.2 0.0 copy-done
  812.2 1.8 fusion.14
  814.1 39.5 %all-gather.1 = f32[12288,8]{0,1:T(8,128)S(1)} all-gather(f32[768,8]{0,1:T(8,128)S(1)} %fusion.14), channel_id=3, replica_groups=mesh['rows'=16,'tp'=16] {'tp'}, dimensions={0}, use_global_device_ids=true | all-gather | bytes 417792 | tf_op jit(solution)/shard_map/all_gather | solution.py:15
  853.6 0.0 copy-done.3
  853.6 4.3 copy.9
  858.0 0.1 copy.7
  858.1 1.0 slice.22
  859.2 4.3 copy.10
  863.5 0.1 copy.8
  863.6 0.9 while.21
  864.6 0.0 copy-start.1
  864.6 3.1 convolution_subtract_fusion
  867.7 0.0 copy-done.1
  867.7 1.8 subtract_subtract_fusion
  869.5 0.0 copy-start.2
  869.5 1.7 copy-done.2
  871.1 1.9 fusion.9
  873.0 75.1 %psum.21 = f32[768,8]{0,1:T(8,128)S(1)} all-reduce(f32[768,8]{0,1:T(8,128)S(1)} %fusion.9), channel_id=1, replica_groups=mesh['rows'=16,'tp'=16] {'tp'}, use_global_device_ids=true, to_apply=%region_5.6 | all-reduce | flops 6144 | bytes 49152 | tf_op jit(solution)/shard_map/psum | solution.py:78
  948.2 0.6 multiply_reduce_fusion
  948.8 4.9 multiply_convert_fusion
  953.7 43.5 %all-reduce = (f32[]{:T(128)}, f32[]{:T(128)}) all-reduce(f32[]{:T(128)} %multiply_reduce_fusion, f32[]{:T(128)} %convert_reduce_fusion), channel_id=1, replica_groups=mesh['rows'=16,'tp'=16] {'rows'}, use_global_device_ids=true, to_apply=%region_7.8 | all-reduce | flops 2 | bytes 16 | tf_op jit(solution)/shard_map/psum | solution.py:84
  (23 shorter events, 0.7 us)
Async XLA Ops:
  7.2 275.2 %all-gather.7.cloned.1.call-start = ((), (), s32[]{:S(2)}) async-start(), calls=%async_computation | async-start | bytes 13369344 | tf_op jit(solution)/shard_map/all_gather | solution.py:57
  7.9 3.4 copy-start.5
  7.9 452.7 %all-gather.9.cloned.1.call-start = ((), (), s32[]{:S(2)}) async-start(), calls=%async_computation.1 | async-start | bytes 17825792 | tf_op jit(solution)/shard_map/all_gather | solution.py:64
  12.1 448.5 %copy-start.6 = (f32[8192]{0:T(1024)S(1)}, f32[8192]{0:T(1024)}, u32[]{:S(2)}) copy-start(f32[8192]{0:T(1024)} %param.8) | copy-start | bytes 98308
  479.4 332.8 %copy-start = (f32[768,1024]{1,0:T(8,128)}, f32[768,1024]{1,0:T(8,128)S(1)}, u32[]{:S(2)}) copy-start(f32[768,1024]{1,0:T(8,128)S(1)} %fusion.18) | copy-start | bytes 9437188
  630.8 222.8 %copy-start.3 = (f32[12288,8]{1,0:T(8,128)}, f32[12288,8]{1,0:T(8,128)S(1)}, u32[]{:S(2)}) copy-start(f32[12288,8]{1,0:T(8,128)S(1)} %all-gather) | copy-start | bytes 1179652
  632.2 142.2 %copy-start.4 = (bf16[768,1024]{1,0:T(8,128)(2,1)S(1)}, bf16[768,1024]{1,0:T(8,128)(2,1)}, u32[]{:S(2)}) copy-start(bf16[768,1024]{1,0:T(8,128)(2,1)} %param.10) | copy-start | bytes 4718596
  864.6 3.1 copy-start.1
  869.5 1.7 copy-start.2
Sparse Core Ops, SparseCore 0:
  9.8 272.4 all-gather.6
  285.1 175.4 all-gather.8
where the time goes:
time: 1010 us
  blocking collectives  478 us (47%)
  waiting for transfers between devices  443 us (44%)
  matrix products  37 us (4%)
  other arithmetic  19.3 us (2%)
  between operations  16.7 us (2%)
  local copies, waits for them, and re-layouts  12.6 us (1%)
    all_gather x4, blocking collectives, merged(): everything = jax.tree.map(lambda part: lax.all_gather(part, axis), shard)  359 us
    all_gather x1, waiting for transfers between devices, body(): gathered = lax.all_gather(teacher_hidden, 'tp', axis=1, tiled=True)  270 us
    all_gather x1, waiting for transfers between devices, body(): lax.all_gather(head_weight, 'rows', axis=0, tiled=True)  171 us
    psum x1, blocking collectives, body(): divergence = lax.psum(partial_value, 'tp')  75.1 us
    psum x1, blocking collectives, body(): loss_sum, len_sum = lax.psum((local_loss, local_len), 'rows')  43.5 us
  transfers between devices with their start and end apart: 2, of which 2 were waited for; matrix products, arithmetic and copies ran while one was open for 1% of the time, Pallas kernels for 0%

commit v1 on v0

v1 whole, which is shorter than its diff:
```python
import jax
import jax.numpy as jnp
from jax import lax
from jax.experimental import pallas as pl
from jax.experimental.pallas import tpu as pltpu
from jax.sharding import PartitionSpec as P

V = 2048
CB = 8
STEPS = 4
NX = 4
NZ = 4
NY = 4
NH = 2
BLOCKS = 16
CHUNK = 128
MIB = 1 << 20


def tp_at(x, z):
    return x * NZ + z


def row_at(h, y, c):
    return h * 2 * NY + y * 2 + c


def x_ring(d):
    return [(tp_at(x, z), tp_at((x + d) % NX, z)) for x in range(NX) for z in range(NZ)]


def z_ring(d):
    return [(tp_at(x, z), tp_at(x, (z + d) % NZ)) for x in range(NX) for z in range(NZ)]


def y_ring(d):
    return [
        (row_at(h, y, c), row_at(h, (y + d) % NY, c))
        for h in range(NH)
        for y in range(NY)
        for c in range(2)
    ]


def row_xor(m):
    return [(r, r ^ m) for r in range(16)]


PAIR = [(t, t ^ 1) for t in range(16)]
SAME_HALF = [[row_at(h, y, c) for y in range(NY) for c in range(2)] for h in range(NH)]


def after(value, *earlier):
    return lax.optimization_barrier((value,) + earlier)[0]


def gather_hidden(own):
    half = own.shape[0] // 2
    blocks = []
    held = own
    gate = ()
    for i in range(NZ):
        nxt = lax.ppermute(held, "tp", z_ring(1)) if i < NZ - 1 else None
        ready = after(held, *gate) if gate else held
        left = lax.ppermute(ready, "tp", x_ring(1))
        right = lax.ppermute(ready, "tp", x_ring(-1))
        top = lax.ppermute(left[:half], "tp", x_ring(1))
        low = lax.ppermute(right[half:], "tp", x_ring(-1))
        blocks += [held, left, right, top, low]
        gate = (left, right)
        held = nxt
    return blocks


def teacher_kernel(slots_ref, gain_ref, student_ref, *refs):
    a_refs, (w_own, w_far) = refs[:20], refs[20:22]
    teach_ref, stats_ref = refs[22:24]
    a_vm, w_vm, square_ref, a_sem, w_sem = refs[24:]
    tok = teach_ref.shape[0]
    half = tok // 2

    for step in range(BLOCKS):
        group = a_refs[5 * (step // 4) : 5 * (step // 4) + 5]
        j = step % 4
        if j < 3:
            pltpu.make_async_copy(group[j], a_vm.at[step], a_sem.at[step]).start()
        else:
            pltpu.make_async_copy(
                group[3], a_vm.at[step, pl.ds(0, half)], a_sem.at[step]
            ).start()
            pltpu.make_async_copy(
                group[4], a_vm.at[step, pl.ds(half, half)], a_sem.at[step]
            ).start()
        slot = slots_ref[step]

        @pl.when(slot < 8)
        def _():
            pltpu.make_async_copy(w_own.at[slot], w_vm.at[step], w_sem.at[step]).start()

        @pl.when(slot >= 8)
        def _():
            pltpu.make_async_copy(w_far.at[slot - 8], w_vm.at[step], w_sem.at[step]).start()

    square_ref[...] = jnp.zeros_like(square_ref)
    teach_ref[...] = jnp.zeros_like(teach_ref)

    def step_body(step, carry):
        pltpu.make_async_copy(a_vm.at[step], a_vm.at[step], a_sem.at[step]).wait()
        pltpu.make_async_copy(w_vm.at[step], w_vm.at[step], w_sem.at[step]).wait()
        gain = gain_ref[slots_ref[BLOCKS + step]]
        for r in range(0, tok, 256):
            wide = a_vm[step, r : r + 256, :].astype(jnp.float32)
            square = wide * wide
            square_ref[r : r + 256, :] += (
                square[:, :128] + square[:, 128:256] + square[:, 256:384] + square[:, 384:]
            )
            normed = (wide * gain).astype(jnp.bfloat16)
            teach_ref[r : r + 256, :] += jnp.dot(
                normed, w_vm[step], preferred_element_type=jnp.float32
            )
        return carry

    lax.fori_loop(0, BLOCKS, step_body, 0)

    lane = lax.broadcasted_iota(jnp.int32, (CHUNK, 128), 1)
    for r in range(0, tok, CHUNK):
        rows = pl.ds(r, CHUNK)
        mean = jnp.sum(square_ref[rows, :], axis=1, keepdims=True) / (BLOCKS * 512)
        teach = teach_ref[rows, :] * lax.rsqrt(mean + 1e-05)
        teach_ref[rows, :] = teach
        stud = student_ref[rows, :].astype(jnp.float32)
        teach_peak = jnp.max(teach, axis=1, keepdims=True)
        stud_peak = jnp.max(stud, axis=1, keepdims=True)
        teach = teach - teach_peak
        stud = stud - stud_peak
        mass = jnp.exp(stud)
        teach_total = jnp.sum(jnp.exp(teach), axis=1, keepdims=True)
        stud_total = jnp.sum(mass, axis=1, keepdims=True)
        cross = jnp.sum(mass * (stud - teach), axis=1, keepdims=True)
        packed = jnp.zeros((CHUNK, 128), jnp.float32)
        for at, value in enumerate((teach_peak, teach_total, stud_peak, stud_total, cross)):
            packed = jnp.where(lane == at, value, packed)
        stats_ref[:, r : r + CHUNK] = packed.T[:8, :]


def teacher_logits(hidden, near, far, gain, student, slots):
    tok, cols = student.shape
    any_space = pl.BlockSpec(memory_space=pl.ANY)
    vmem = pl.BlockSpec(memory_space=pltpu.VMEM)
    return pl.pallas_call(
        teacher_kernel,
        out_shape=(
            jax.ShapeDtypeStruct((tok, cols), jnp.float32),
            jax.ShapeDtypeStruct((8, tok), jnp.float32),
        ),
        in_specs=[pl.BlockSpec(memory_space=pltpu.SMEM), vmem, vmem] + [any_space] * 22,
        out_specs=(vmem, vmem),
        scratch_shapes=[
            pltpu.VMEM((BLOCKS, tok, 512), jnp.bfloat16),
            pltpu.VMEM((BLOCKS, 512, cols), jnp.bfloat16),
            pltpu.VMEM((tok, 128), jnp.float32),
            pltpu.SemaphoreType.DMA((BLOCKS,)),
            pltpu.SemaphoreType.DMA((BLOCKS,)),
        ],
        compiler_params=pltpu.CompilerParams(vmem_limit_bytes=52 * MIB),
        name="teacher",
    )(slots, gain.reshape(BLOCKS, 1, 512), student, *hidden, near, far)


def grad_kernel(coef_ref, teach_ref, student_ref, grad_ref):
    coef = coef_ref[...].T
    stud = student_ref[...].astype(jnp.float32)
    prob = jnp.exp((stud - coef[:, 0:1]) - coef[:, 1:2])
    differ = (stud - teach_ref[...]) - coef[:, 2:3]
    grad_ref[...] = ((coef[:, 3:4] * prob) * differ).astype(jnp.bfloat16)


def gradient(coef, teach, student):
    tok, cols = student.shape
    tile = 256
    return pl.pallas_call(
        grad_kernel,
        grid=(tok // tile,),
        out_shape=jax.ShapeDtypeStruct((tok, cols), jnp.bfloat16),
        in_specs=[
            pl.BlockSpec((8, tile), lambda i: (0, i)),
            pl.BlockSpec((tile, cols), lambda i: (i, 0)),
            pl.BlockSpec((tile, cols), lambda i: (i, 0)),
        ],
        out_specs=pl.BlockSpec((tile, cols), lambda i: (i, 0)),
        compiler_params=pltpu.CompilerParams(vmem_limit_bytes=32 * MIB),
        name="gradient",
    )(coef, teach, student)


def total_everywhere(value):
    for axis, moves in (
        ("rows", [row_xor(m) for m in (1, 8, 9)]),
        ("tp", [z_ring(d) for d in (1, 2, 3)]),
        ("rows", [y_ring(d) for d in (1, 2, 3)]),
        ("tp", [x_ring(d) for d in (1, 2, 3)]),
    ):
        first, second, third = [lax.ppermute(value, axis, m) for m in moves]
        value = (value + first) + (second + third)
    return value


def body(teacher_hidden, norm_gain, head_weight, student_logits, row_lengths):
    tok = teacher_hidden.shape[0]
    far_shard = lax.ppermute(head_weight, "rows", row_xor(8))
    near = lax.all_gather(head_weight, "rows", axis_index_groups=SAME_HALF)
    far = lax.all_gather(far_shard, "rows", axis_index_groups=SAME_HALF)
    hidden = gather_hidden(teacher_hidden)

    tp = lax.axis_index("tp")
    half = lax.axis_index("rows") // 8
    z_off = jnp.arange(BLOCKS, dtype=jnp.int32) // 4
    x_off = jnp.asarray([0, 1, 3, 2] * 4, jnp.int32)
    block = ((tp // NZ - x_off) % NX) * NZ + (tp % NZ - z_off) % NZ
    slot = jnp.where(block // 8 == half, block % 8, 8 + block % 8)
    slots = jnp.concatenate([slot, block]).astype(jnp.int32)
    teach, stats = teacher_logits(hidden, near, far, norm_gain, student_logits, slots)

    other = lax.ppermute(stats, "tp", PAIR)
    teach_peak = jnp.maximum(stats[0], other[0])
    stud_peak = jnp.maximum(stats[2], other[2])
    teach_total = stud_total = cross = 0.0
    for part in (stats, other):
        teach_low = part[0] - teach_peak
        stud_low = part[2] - stud_peak
        weight = jnp.exp(stud_low)
        teach_total = teach_total + jnp.exp(teach_low) * part[1]
        stud_total = stud_total + weight * part[3]
        cross = cross + weight * (part[4] + part[3] * (stud_low - teach_low))
    log_stud = jnp.log(stud_total)
    log_teach = jnp.log(teach_total)
    divergence = cross / stud_total - (log_stud - log_teach)
    steps_of = jnp.arange(tok, dtype=jnp.int32) % STEPS
    live = (steps_of < jnp.repeat(row_lengths, STEPS)).astype(jnp.float32)
    offset = (stud_peak - teach_peak) + (log_stud - log_teach) + divergence
    none = jnp.zeros_like(live)
    coef = jnp.stack([stud_peak, log_stud, offset, V * live, none, none, none, none])
    grad = gradient(coef, teach, student_logits)

    sums = jnp.stack([jnp.sum(live * divergence), jnp.sum(row_lengths.astype(jnp.float32))])
    sums = total_everywhere(sums.reshape(1, 2))
    loss = (0.5 * sums[0, 0]) / (CB * (sums[0, 1] / BLOCKS))
    return (grad, loss)


def solution(mesh):
    in_specs = (P("rows", "tp"), P(), P("rows", "tp"), P("rows", "tp"), P("rows"))
    out_specs = (P("rows", "tp"), P())
    return jax.shard_map(body, mesh=mesh, in_specs=in_specs, out_specs=out_specs, check_vma=False)
```

time: 1010 us -> 250 us (0.25)
  blocking collectives: 478 us -> 0 us
  waiting for transfers between devices: 443 us -> 130 us
  starting transfers between devices: 0.08 us -> 59 us
  matrix products: 37 us -> 0 us
  Pallas kernels: 0 us -> 25.7 us
  other arithmetic: 19.3 us -> 6.44 us
    all_gather x2, waiting for transfers between devices: 441 us -> 0.01 us  [the longest x1 0.01 us: body(): near = lax.all_gather(head_weight, 'rows', axis_index_groups=SAME_HALF)]
    all_gather x4 -> x0, blocking collectives: 359 us -> none  [merged(): everything = jax.tree.map(lambda part: lax.all_gather(part, axis), shard)]
    ppermute x0 -> x33, waiting for transfers between devices: none -> 129 us  [the longest x4 46.7 us: gather_hidden(): left = lax.ppermute(ready, 'tp', x_ring(1))]
    psum x2 -> x0, blocking collectives: 119 us -> none  [the longest x1 75.1 us: body(): divergence = lax.psum(partial_value, 'tp')]
    ppermute x0 -> x33, starting transfers between devices: none -> 58.9 us  [the longest x12 23.2 us: total_everywhere(): first, second, third = [lax.ppermute(value, axis, m) for m in moves]]
    dot_general x9 -> x0, matrix products: 37 us -> none  [the longest x1 18.8 us: body(): jnp.dot(normed, lax.all_gather(head_weight, 'rows', axis=0, tiled=True),...]
    pallas_call x0 -> x2, Pallas kernels: none -> 25.7 us  [the longest x1 23 us: teacher_logits(): pl.pallas_call(teacher_kernel, out_shape=(jax.ShapeDtypeStruct((tok, cols...]
  transfers between devices with their start and end apart: 2 -> 35, of which waited for: 2 -> 21; matrix products, arithmetic and copies ran while one was open for 1% -> 3% of each run, Pallas kernels for 0% -> 1%
where the time goes in v1:
time: 250 us; the launch traced here: 248 us
  waiting for transfers between devices  130 us (52%)
  starting transfers between devices  59 us (24%)
  Pallas kernels  25.7 us (10%)
  between operations  16.7 us (7%)
  local copies, waits for them, and re-layouts  9.95 us (4%)
  other arithmetic  6.44 us (3%)
    ppermute x4, waiting for transfers between devices, gather_hidden(): left = lax.ppermute(ready, 'tp', x_ring(1))  46.7 us
    ppermute x1, waiting for transfers between devices, body(): far_shard = lax.ppermute(head_weight, 'rows', row_xor(8))  44.7 us
    ppermute x12, starting transfers between devices, total_everywhere(): first, second, third = [lax.ppermute(value, axis, m) for m in moves]  23.2 us
    pallas_call x1, Pallas kernels, teacher_logits(): pl.pallas_call(teacher_kernel, out_shape=(jax.ShapeDtypeStruct((tok, cols...  23 us
    ppermute x4, waiting for transfers between devices, gather_hidden(): top = lax.ppermute(left[:half], 'tp', x_ring(1))  15 us
    ppermute x4, starting transfers between devices, gather_hidden(): low = lax.ppermute(right[half:], 'tp', x_ring(-1))  12.9 us
    ppermute x3, waiting for transfers between devices, gather_hidden(): nxt = lax.ppermute(held, 'tp', z_ring(1)) if i < NZ - 1 else None  12 us
    ppermute x1, starting transfers between devices, body(): far_shard = lax.ppermute(head_weight, 'rows', row_xor(8))  7.28 us
  transfers between devices with their start and end apart: 35, of which 21 were waited for; matrix products, arithmetic and copies ran while one was open for 3% of the time, Pallas kernels for 1%

profile of v1, /device:TPU:2, one launch (start us, length us, event | category | flops | bytes accessed | tf_op | source)
XLA Modules:
  0.0 247.6 jit_solution(2208100486439968132)
XLA Ops:
  7.2 0.7 all-gather.5.cloned.1.call-update
  7.9 7.3 %collective-permute-start.19 = (bf16[512,1024]{1,0:T(8,128)(2,1)}, bf16[512,1024]{1,0:T(8,128)(2,1)S(1)}, u32[]{:S(2)}, u32[]{:S(2)}) collective-permute-start(bf16[512,1024]{1,0:T(8,128)(2,1)} %param.8), channel_id=1, source_target_pairs={{0,128},{16,144},{32,160},{48,176},{64,192},{80,208},{96,224},{112... | collective-permute-start | bytes 3145736 | tf_op jit(solution)/shard_map/ppermute | solution.py:210
  15.2 44.7 %collective-permute-done.19 = bf16[512,1024]{1,0:T(8,128)(2,1)S(1)} collective-permute-done((bf16[512,1024]{1,0:T(8,128)(2,1)}, bf16[512,1024]{1,0:T(8,128)(2,1)S(1)}, u32[]{:S(2)}, u32[]{:S(2)}) %collective-permute-start.19) | collective-permute-done | bytes 1048608 | tf_op jit(solution)/shard_map/ppermute | solution.py:210
  59.9 1.0 copy-done.9
  60.9 1.6 collective-permute-start
  62.5 0.5 collective-permute-start.1
  63.0 2.4 collective-permute-start.4
  65.4 7.8 %collective-permute-done.refs_1_ = bf16[768,512]{1,0:T(8,128)(2,1)S(1)} collective-permute-done((bf16[768,512]{1,0:T(8,128)(2,1)}, bf16[768,512]{1,0:T(8,128)(2,1)S(1)}, u32[]{:S(2)}, u32[]{:S(2)}) %collective-permute-start) | collective-permute-done | bytes 786464 | tf_op jit(solution)/shard_map/ppermute | solution.py:65
  73.2 1.5 collective-permute-done.1.refs_2_
  74.7 6.6 %collective-permute-done.4.refs_5_ = bf16[768,512]{1,0:T(8,128)(2,1)S(1)} collective-permute-done((bf16[768,512]{1,0:T(8,128)(2,1)}, bf16[768,512]{1,0:T(8,128)(2,1)S(1)}, u32[]{:S(2)}, u32[]{:S(2)}) %collective-permute-start.4) | collective-permute-done | bytes 786464 | tf_op jit(solution)/shard_map/ppermute | solution.py:63
  81.3 1.5 collective-permute-start.5
  82.8 0.5 collective-permute-start.6
  83.3 2.4 collective-permute-start.9
  85.7 12.7 %collective-permute-done.5.refs_6_ = bf16[768,512]{1,0:T(8,128)(2,1)S(1)} collective-permute-done((bf16[768,512]{1,0:T(8,128)(2,1)S(1)}, bf16[768,512]{1,0:T(8,128)(2,1)S(1)}, u32[]{:S(2)}, u32[]{:S(2)}) %collective-permute-start.5) | collective-permute-done | bytes 786464 | tf_op jit(solution)/shard_map/ppermute | solution.py:65
  98.4 1.2 collective-permute-done.6.refs_7_
  99.6 2.1 collective-permute-done.9.refs_10_
  101.6 1.5 collective-permute-start.10
  103.1 1.5 collective-permute-start.11
  104.6 0.6 collective-permute-start.14
  105.2 13.3 %collective-permute-done.10.refs_11_ = bf16[768,512]{1,0:T(8,128)(2,1)S(1)} collective-permute-done((bf16[768,512]{1,0:T(8,128)(2,1)S(1)}, bf16[768,512]{1,0:T(8,128)(2,1)S(1)}, u32[]{:S(2)}, u32[]{:S(2)}) %collective-permute-start.10) | collective-permute-done | bytes 786464 | tf_op jit(solution)/shard_map/ppermute | solution.py:65
  118.5 3.3 %collective-permute-done.14.refs_15_ = bf16[768,512]{1,0:T(8,128)(2,1)} collective-permute-done((bf16[768,512]{1,0:T(8,128)(2,1)S(1)}, bf16[768,512]{1,0:T(8,128)(2,1)}, u32[]{:S(2)}, u32[]{:S(2)}) %collective-permute-start.14) | collective-permute-done | bytes 786464 | tf_op jit(solution)/shard_map/ppermute | solution.py:63
  122.1 2.7 %collective-permute-start.16 = (bf16[768,512]{1,0:T(8,128)(2,1)}, bf16[768,512]{1,0:T(8,128)(2,1)}, u32[]{:S(2)}, u32[]{:S(2)}) collective-permute-start(bf16[768,512]{1,0:T(8,128)(2,1)} %collective-permute-done.14.refs_15_), channel_id=1, source_target_pairs={{0,12},{1,13},{2,14},{3,15},{4,0},{5,1},{6,2},{7,3},{8,4},{9,5},{1... | collective-permute-start | bytes 2359304 | tf_op jit(solution)/shard_map/ppermute | solution.py:66
  124.8 0.8 slice.86
  125.5 0.8 slice.87
  126.3 3.2 %collective-permute-start.3 = (bf16[384,512]{1,0:T(8,128)(2,1)}, bf16[384,512]{1,0:T(8,128)(2,1)S(1)}, u32[]{:S(2)}, u32[]{:S(2)}) collective-permute-start(bf16[384,512]{1,0:T(8,128)(2,1)} %slice.87), channel_id=1, source_target_pairs={{0,12},{1,13},{2,14},{3,15},{4,0},{5,1},{6,2},{7,3},{8,4},{9,5},{1... | collective-permute-start | bytes 1179656 | tf_op jit(solution)/shard_map/ppermute | solution.py:68
  129.6 0.8 slice.88
  130.5 13.0 %collective-permute-done.15.refs_16_ = bf16[768,512]{1,0:T(8,128)(2,1)} collective-permute-done((bf16[768,512]{1,0:T(8,128)(2,1)}, bf16[768,512]{1,0:T(8,128)(2,1)}, u32[]{:S(2)}, u32[]{:S(2)}) %collective-permute-start.15) | collective-permute-done | bytes 786464 | tf_op jit(solution)/shard_map/ppermute | solution.py:65
  143.5 3.2 %collective-permute-start.8 = (bf16[384,512]{1,0:T(8,128)(2,1)S(1)}, bf16[384,512]{1,0:T(8,128)(2,1)S(1)}, u32[]{:S(2)}, u32[]{:S(2)}) collective-permute-start(bf16[384,512]{1,0:T(8,128)(2,1)S(1)} %slice.89), channel_id=1, source_target_pairs={{0,12},{1,13},{2,14},{3,15},{4,0},{5,1},{6,2},{7,3},{8,4},{9,5},{1... | collective-permute-start | bytes 1179656 | tf_op jit(solution)/shard_map/ppermute | solution.py:68
  146.8 1.0 slice.92
  147.9 1.0 slice.93
  148.9 2.9 %collective-permute-done.2.refs_3_ = bf16[384,512]{1,0:T(8,128)(2,1)S(1)} collective-permute-done((bf16[384,512]{1,0:T(8,128)(2,1)}, bf16[384,512]{1,0:T(8,128)(2,1)S(1)}, u32[]{:S(2)}, u32[]{:S(2)}) %collective-permute-start.2) | collective-permute-done | bytes 393248 | tf_op jit(solution)/shard_map/ppermute | solution.py:67
  151.9 3.2 %collective-permute-start.13 = (bf16[384,512]{1,0:T(8,128)(2,1)S(1)}, bf16[384,512]{1,0:T(8,128)(2,1)}, u32[]{:S(2)}, u32[]{:S(2)}) collective-permute-start(bf16[384,512]{1,0:T(8,128)(2,1)S(1)} %slice.91), channel_id=1, source_target_pairs={{0,12},{1,13},{2,14},{3,15},{4,0},{5,1},{6,2},{7,3},{8,4},{9,5},{1... | collective-permute-start | bytes 1179656 | tf_op jit(solution)/shard_map/ppermute | solution.py:68
  155.1 5.2 %collective-permute-done.7.refs_8_ = bf16[384,512]{1,0:T(8,128)(2,1)S(1)} collective-permute-done((bf16[384,512]{1,0:T(8,128)(2,1)}, bf16[384,512]{1,0:T(8,128)(2,1)S(1)}, u32[]{:S(2)}, u32[]{:S(2)}) %collective-permute-start.7) | collective-permute-done | bytes 393248 | tf_op jit(solution)/shard_map/ppermute | solution.py:67
  160.3 3.2 %collective-permute-start.18 = (bf16[384,512]{1,0:T(8,128)(2,1)S(1)}, bf16[384,512]{1,0:T(8,128)(2,1)}, u32[]{:S(2)}, u32[]{:S(2)}) collective-permute-start(bf16[384,512]{1,0:T(8,128)(2,1)S(1)} %slice.93), channel_id=1, source_target_pairs={{0,12},{1,13},{2,14},{3,15},{4,0},{5,1},{6,2},{7,3},{8,4},{9,5},{1... | collective-permute-start | bytes 1179656 | tf_op jit(solution)/shard_map/ppermute | solution.py:68
  163.6 0.7 multiply_add_fusion
  164.3 2.6 %collective-permute-done.12.refs_13_ = bf16[384,512]{1,0:T(8,128)(2,1)S(1)} collective-permute-done((bf16[384,512]{1,0:T(8,128)(2,1)S(1)}, bf16[384,512]{1,0:T(8,128)(2,1)S(1)}, u32[]{:S(2)}, u32[]{:S(2)}) %collective-permute-start.12) | collective-permute-done | bytes 393248 | tf_op jit(solution)/shard_map/ppermute | solution.py:67
  166.8 4.3 %collective-permute-done.17.refs_18_ = bf16[384,512]{1,0:T(8,128)(2,1)} collective-permute-done((bf16[384,512]{1,0:T(8,128)(2,1)S(1)}, bf16[384,512]{1,0:T(8,128)(2,1)}, u32[]{:S(2)}, u32[]{:S(2)}) %collective-permute-start.17) | collective-permute-done | bytes 393248 | tf_op jit(solution)/shard_map/ppermute | solution.py:67
  171.2 0.8 copy-done.2
  171.9 23.0 %teacher.1 = (f32[768,1024]{1,0:T(8,128)}, f32[8,768]{1,0:T(8,128)}) custom-call(s32[32]{0:T(128)S(1)} %pad_add_fusion.slots_ref, f32[16,1,512]{2,1,0:T(1,128)S(1)} %bitcast.10, bf16[768,1024]{1,0:T(8,128)(2,1)} %student_ref.3, bf16[768,512]{1,0:T(8,128)(2,1)} %refs_0_.1, bf16[768,512]{1,0:T(8,128)(2,1)} %copy-done.3, bf16[768,512]{1,0:T(8,128)(2,1)} %copy-done.4, ...), custom_call_target="tpu_custom_call" | custom-call | tf_op jit(solution)/shard_map/teacher/pallas_call | solution.py:150
  195.1 0.6 convert_reduce_fusion
  195.7 1.0 iota.30
  196.9 2.2 collective-permute-done.20
  199.1 1.6 fusion.4
  200.7 1.3 maximum_bitcast_fusion
  202.0 4.5 %collective-permute-start.22 = (f32[1,2]{1,0:T(1,128)S(1)}, f32[1,2]{1,0:T(1,128)S(1)}, u32[]{:S(2)}, u32[]{:S(2)}) collective-permute-start(f32[1,2]{1,0:T(1,128)S(1)} %maximum_bitcast_fusion), channel_id=1, source_target_pairs={{0,128},{16,144},{32,160},{48,176},{64,192},{80,208},{96,224},{112... | collective-permute-start | bytes 32 | tf_op jit(solution)/shard_map/ppermute | solution.py:203
  206.6 1.3 collective-permute-start.23
  207.8 0.8 add_add_fusion
  208.7 1.9 copy-done.1
  210.5 2.7 %gradient.1 = bf16[768,1024]{1,0:T(8,128)(2,1)} custom-call(f32[8,768]{1,0:T(8,128)S(1)} %stack.20.coef_ref, f32[768,1024]{1,0:T(8,128)S(1)} %copy-done.1, bf16[768,1024]{1,0:T(8,128)(2,1)S(1)} %copy-done), custom_call_target="tpu_custom_call" | custom-call | tf_op jit(solution)/shard_map/gradient/pallas_call | solution.py:181
  213.4 1.4 add_add_fusion.4
  214.8 2.0 collective-permute-start.25
  216.8 1.8 collective-permute-start.26
  218.6 1.5 collective-permute-done.24
  220.1 0.6 collective-permute-done.26
  220.7 1.6 collective-permute-start.27
  222.3 2.9 %collective-permute-start.28 = (f32[1,2]{1,0:T(1,128)S(1)}, f32[1,2]{1,0:T(1,128)S(1)}, u32[]{:S(2)}, u32[]{:S(2)}) collective-permute-start(f32[1,2]{1,0:T(1,128)S(1)} %add_add_fusion.3), channel_id=1, source_target_pairs={{0,64},{16,80},{32,96},{48,112},{64,0},{80,16},{96,32},{112,48},{1... | collective-permute-start | bytes 32 | tf_op jit(solution)/shard_map/ppermute | solution.py:203
  225.2 1.3 collective-permute-start.29
  226.5 0.8 collective-permute-done.28
  227.3 1.4 collective-permute-done.29
  228.7 2.4 collective-permute-start.30
  231.1 3.0 %collective-permute-start.31 = (f32[1,2]{1,0:T(1,128)S(1)}, f32[1,2]{1,0:T(1,128)S(1)}, u32[]{:S(2)}, u32[]{:S(2)}) collective-permute-start(f32[1,2]{1,0:T(1,128)S(1)} %add_add_fusion.2), channel_id=1, source_target_pairs={{0,8},{1,9},{2,10},{3,11},{4,12},{5,13},{6,14},{7,15},{8,0},{9,1},... | collective-permute-start | bytes 32 | tf_op jit(solution)/shard_map/ppermute | solution.py:203
  234.1 2.3 collective-permute-start.32
  236.4 1.3 collective-permute-done.32
  237.7 0.6 fusion.11
  (64 shorter events, 1.3 us)
Async XLA Ops:
  7.2 164.0 %all-gather.5.cloned.1.call-start = ((), (), s32[]{:S(2)}) async-start(), calls=%async_computation | async-start | bytes 9437184 | tf_op jit(solution)/shard_map/all_gather | solution.py:211
  7.9 163.3 %all-gather.7.cloned.1.call-start = ((), (), s32[]{:S(2)}) async-start(), calls=%async_computation.1 | async-start | bytes 9437184 | tf_op jit(solution)/shard_map/all_gather | solution.py:212
  7.9 52.0 %collective-permute-start.19 = (bf16[512,1024]{1,0:T(8,128)(2,1)}, bf16[512,1024]{1,0:T(8,128)(2,1)S(1)}, u32[]{:S(2)}, u32[]{:S(2)}) collective-permute-start(bf16[512,1024]{1,0:T(8,128)(2,1)} %param.8), channel_id=1, source_target_pairs={{0,128},{16,144},{32,160},{48,176},{64,192},{80,208},{96,224},{112... | collective-permute-start | bytes 3145736 | tf_op jit(solution)/shard_map/ppermute | solution.py:210
  59.9 1.0 copy-start.9
  60.9 102.6 %copy-start.13 = (s32[16]{0:T(128)S(1)}, s32[16]{0:T(128)}, u32[]{:S(2)}) copy-start(s32[16]{0:T(128)} %constant.118) | copy-start | bytes 196
  60.9 12.3 %collective-permute-start = (bf16[768,512]{1,0:T(8,128)(2,1)}, bf16[768,512]{1,0:T(8,128)(2,1)S(1)}, u32[]{:S(2)}, u32[]{:S(2)}) collective-permute-start(bf16[768,512]{1,0:T(8,128)(2,1)} %refs_0_.1), channel_id=1, source_target_pairs={{0,4},{1,5},{2,6},{3,7},{4,8},{5,9},{6,10},{7,11},{8,12},{9,13},{1... | collective-permute-start | bytes 2359304 | tf_op jit(solution)/shard_map/ppermute | solution.py:65
  62.5 12.2 %collective-permute-start.1 = (bf16[768,512]{1,0:T(8,128)(2,1)}, bf16[768,512]{1,0:T(8,128)(2,1)S(1)}, u32[]{:S(2)}, u32[]{:S(2)}) collective-permute-start(bf16[768,512]{1,0:T(8,128)(2,1)} %refs_0_.1), channel_id=1, source_target_pairs={{0,12},{1,13},{2,14},{3,15},{4,0},{5,1},{6,2},{7,3},{8,4},{9,5},{1... | collective-permute-start | bytes 2359304 | tf_op jit(solution)/shard_map/ppermute | solution.py:66
  63.0 18.2 %collective-permute-start.4 = (bf16[768,512]{1,0:T(8,128)(2,1)}, bf16[768,512]{1,0:T(8,128)(2,1)S(1)}, u32[]{:S(2)}, u32[]{:S(2)}) collective-permute-start(bf16[768,512]{1,0:T(8,128)(2,1)} %refs_0_.1), channel_id=1, source_target_pairs={{0,1},{1,2},{2,3},{3,0},{4,5},{5,6},{6,7},{7,4},{8,9},{9,10},{10,1... | collective-permute-start | bytes 2359304 | tf_op jit(solution)/shard_map/ppermute | solution.py:63
  73.2 56.4 %copy-start.3 = (bf16[768,512]{1,0:T(8,128)(2,1)}, bf16[768,512]{1,0:T(8,128)(2,1)S(1)}, u32[]{:S(2)}) copy-start(bf16[768,512]{1,0:T(8,128)(2,1)S(1)} %collective-permute-done.refs_1_) | copy-start | bytes 2359300
  74.7 55.6 %copy-start.4 = (bf16[768,512]{1,0:T(8,128)(2,1)}, bf16[768,512]{1,0:T(8,128)(2,1)S(1)}, u32[]{:S(2)}) copy-start(bf16[768,512]{1,0:T(8,128)(2,1)S(1)} %collective-permute-done.1.refs_2_) | copy-start | bytes 2359300
  81.3 37.2 %copy-start.10 = (bf16[768,512]{1,0:T(8,128)(2,1)}, bf16[768,512]{1,0:T(8,128)(2,1)S(1)}, u32[]{:S(2)}) copy-start(bf16[768,512]{1,0:T(8,128)(2,1)S(1)} %collective-permute-done.4.refs_5_) | copy-start | bytes 2359300
  81.3 17.1 %collective-permute-start.5 = (bf16[768,512]{1,0:T(8,128)(2,1)S(1)}, bf16[768,512]{1,0:T(8,128)(2,1)S(1)}, u32[]{:S(2)}, u32[]{:S(2)}) collective-permute-start(bf16[768,512]{1,0:T(8,128)(2,1)S(1)} %collective-permute-done.4.refs_5_), channel_id=1, source_target_pairs={{0,4},{1,5},{2,6},{3,7},{4,8},{5,9},{6,10},{7,11},{8,12},{9,13},{1... | collective-permute-start | bytes 2359304 | tf_op jit(solution)/shard_map/ppermute | solution.py:65
  82.8 16.8 %collective-permute-start.6 = (bf16[768,512]{1,0:T(8,128)(2,1)S(1)}, bf16[768,512]{1,0:T(8,128)(2,1)S(1)}, u32[]{:S(2)}, u32[]{:S(2)}) collective-permute-start(bf16[768,512]{1,0:T(8,128)(2,1)S(1)} %collective-permute-done.4.refs_5_), channel_id=1, source_target_pairs={{0,12},{1,13},{2,14},{3,15},{4,0},{5,1},{6,2},{7,3},{8,4},{9,5},{1... | collective-permute-start | bytes 2359304 | tf_op jit(solution)/shard_map/ppermute | solution.py:66
  83.3 18.3 %collective-permute-start.9 = (bf16[768,512]{1,0:T(8,128)(2,1)S(1)}, bf16[768,512]{1,0:T(8,128)(2,1)S(1)}, u32[]{:S(2)}, u32[]{:S(2)}) collective-permute-start(bf16[768,512]{1,0:T(8,128)(2,1)S(1)} %collective-permute-done.4.refs_5_), channel_id=1, source_target_pairs={{0,1},{1,2},{2,3},{3,0},{4,5},{5,6},{6,7},{7,4},{8,9},{9,10},{10,1... | collective-permute-start | bytes 2359304 | tf_op jit(solution)/shard_map/ppermute | solution.py:63
  98.4 32.0 %copy-start.5 = (bf16[768,512]{1,0:T(8,128)(2,1)}, bf16[768,512]{1,0:T(8,128)(2,1)S(1)}, u32[]{:S(2)}) copy-start(bf16[768,512]{1,0:T(8,128)(2,1)S(1)} %collective-permute-done.5.refs_6_) | copy-start | bytes 2359300
  99.6 49.3 %copy-start.6 = (bf16[768,512]{1,0:T(8,128)(2,1)}, bf16[768,512]{1,0:T(8,128)(2,1)S(1)}, u32[]{:S(2)}) copy-start(bf16[768,512]{1,0:T(8,128)(2,1)S(1)} %collective-permute-done.6.refs_7_) | copy-start | bytes 2359300
  101.6 23.1 %copy-start.11 = (bf16[768,512]{1,0:T(8,128)(2,1)}, bf16[768,512]{1,0:T(8,128)(2,1)S(1)}, u32[]{:S(2)}) copy-start(bf16[768,512]{1,0:T(8,128)(2,1)S(1)} %collective-permute-done.9.refs_10_) | copy-start | bytes 2359300
  101.6 16.8 %collective-permute-start.10 = (bf16[768,512]{1,0:T(8,128)(2,1)S(1)}, bf16[768,512]{1,0:T(8,128)(2,1)S(1)}, u32[]{:S(2)}, u32[]{:S(2)}) collective-permute-start(bf16[768,512]{1,0:T(8,128)(2,1)S(1)} %collective-permute-done.9.refs_10_), channel_id=1, source_target_pairs={{0,4},{1,5},{2,6},{3,7},{4,8},{5,9},{6,10},{7,11},{8,12},{9,13},{1... | collective-permute-start | bytes 2359304 | tf_op jit(solution)/shard_map/ppermute | solution.py:65
  103.1 15.3 %collective-permute-start.11 = (bf16[768,512]{1,0:T(8,128)(2,1)S(1)}, bf16[768,512]{1,0:T(8,128)(2,1)S(1)}, u32[]{:S(2)}, u32[]{:S(2)}) collective-permute-start(bf16[768,512]{1,0:T(8,128)(2,1)S(1)} %collective-permute-done.9.refs_10_), channel_id=1, source_target_pairs={{0,12},{1,13},{2,14},{3,15},{4,0},{5,1},{6,2},{7,3},{8,4},{9,5},{1... | collective-permute-start | bytes 2359304 | tf_op jit(solution)/shard_map/ppermute | solution.py:66
  104.6 17.2 %collective-permute-start.14 = (bf16[768,512]{1,0:T(8,128)(2,1)S(1)}, bf16[768,512]{1,0:T(8,128)(2,1)}, u32[]{:S(2)}, u32[]{:S(2)}) collective-permute-start(bf16[768,512]{1,0:T(8,128)(2,1)S(1)} %collective-permute-done.9.refs_10_), channel_id=1, source_target_pairs={{0,1},{1,2},{2,3},{3,0},{4,5},{5,6},{6,7},{7,4},{8,9},{9,10},{10,1... | collective-permute-start | bytes 2359304 | tf_op jit(solution)/shard_map/ppermute | solution.py:63
  118.4 30.5 %copy-start.7 = (bf16[768,512]{1,0:T(8,128)(2,1)}, bf16[768,512]{1,0:T(8,128)(2,1)S(1)}, u32[]{:S(2)}) copy-start(bf16[768,512]{1,0:T(8,128)(2,1)S(1)} %collective-permute-done.10.refs_11_) | copy-start | bytes 2359300
  118.4 12.0 %copy-start.8 = (bf16[768,512]{1,0:T(8,128)(2,1)}, bf16[768,512]{1,0:T(8,128)(2,1)S(1)}, u32[]{:S(2)}) copy-start(bf16[768,512]{1,0:T(8,128)(2,1)S(1)} %collective-permute-done.11.refs_12_) | copy-start | bytes 2359300
  121.8 21.7 %collective-permute-start.15 = (bf16[768,512]{1,0:T(8,128)(2,1)}, bf16[768,512]{1,0:T(8,128)(2,1)}, u32[]{:S(2)}, u32[]{:S(2)}) collective-permute-start(bf16[768,512]{1,0:T(8,128)(2,1)} %collective-permute-done.14.refs_15_), channel_id=1, source_target_pairs={{0,4},{1,5},{2,6},{3,7},{4,8},{5,9},{6,10},{7,11},{8,12},{9,13},{1... | collective-permute-start | bytes 2359304 | tf_op jit(solution)/shard_map/ppermute | solution.py:65
  122.1 25.7 %collective-permute-start.16 = (bf16[768,512]{1,0:T(8,128)(2,1)}, bf16[768,512]{1,0:T(8,128)(2,1)}, u32[]{:S(2)}, u32[]{:S(2)}) collective-permute-start(bf16[768,512]{1,0:T(8,128)(2,1)} %collective-permute-done.14.refs_15_), channel_id=1, source_target_pairs={{0,12},{1,13},{2,14},{3,15},{4,0},{5,1},{6,2},{7,3},{8,4},{9,5},{1... | collective-permute-start | bytes 2359304 | tf_op jit(solution)/shard_map/ppermute | solution.py:66
  125.5 26.3 %collective-permute-start.2 = (bf16[384,512]{1,0:T(8,128)(2,1)}, bf16[384,512]{1,0:T(8,128)(2,1)S(1)}, u32[]{:S(2)}, u32[]{:S(2)}) collective-permute-start(bf16[384,512]{1,0:T(8,128)(2,1)} %slice.86), channel_id=1, source_target_pairs={{0,4},{1,5},{2,6},{3,7},{4,8},{5,9},{6,10},{7,11},{8,12},{9,13},{1... | collective-permute-start | bytes 1179656 | tf_op jit(solution)/shard_map/ppermute | solution.py:67
  126.3 28.8 %collective-permute-start.3 = (bf16[384,512]{1,0:T(8,128)(2,1)}, bf16[384,512]{1,0:T(8,128)(2,1)S(1)}, u32[]{:S(2)}, u32[]{:S(2)}) collective-permute-start(bf16[384,512]{1,0:T(8,128)(2,1)} %slice.87), channel_id=1, source_target_pairs={{0,12},{1,13},{2,14},{3,15},{4,0},{5,1},{6,2},{7,3},{8,4},{9,5},{1... | collective-permute-start | bytes 1179656 | tf_op jit(solution)/shard_map/ppermute | solution.py:68
  130.3 29.9 %collective-permute-start.7 = (bf16[384,512]{1,0:T(8,128)(2,1)}, bf16[384,512]{1,0:T(8,128)(2,1)S(1)}, u32[]{:S(2)}, u32[]{:S(2)}) collective-permute-start(bf16[384,512]{1,0:T(8,128)(2,1)} %slice.88), channel_id=1, source_target_pairs={{0,4},{1,5},{2,6},{3,7},{4,8},{5,9},{6,10},{7,11},{8,12},{9,13},{1... | collective-permute-start | bytes 1179656 | tf_op jit(solution)/shard_map/ppermute | solution.py:67
  143.5 20.7 %collective-permute-start.8 = (bf16[384,512]{1,0:T(8,128)(2,1)S(1)}, bf16[384,512]{1,0:T(8,128)(2,1)S(1)}, u32[]{:S(2)}, u32[]{:S(2)}) collective-permute-start(bf16[384,512]{1,0:T(8,128)(2,1)S(1)} %slice.89), channel_id=1, source_target_pairs={{0,12},{1,13},{2,14},{3,15},{4,0},{5,1},{6,2},{7,3},{8,4},{9,5},{1... | collective-permute-start | bytes 1179656 | tf_op jit(solution)/shard_map/ppermute | solution.py:68
  147.8 19.0 %collective-permute-start.12 = (bf16[384,512]{1,0:T(8,128)(2,1)S(1)}, bf16[384,512]{1,0:T(8,128)(2,1)S(1)}, u32[]{:S(2)}, u32[]{:S(2)}) collective-permute-start(bf16[384,512]{1,0:T(8,128)(2,1)S(1)} %slice.90), channel_id=1, source_target_pairs={{0,4},{1,5},{2,6},{3,7},{4,8},{5,9},{6,10},{7,11},{8,12},{9,13},{1... | collective-permute-start | bytes 1179656 | tf_op jit(solution)/shard_map/ppermute | solution.py:67
  151.9 15.0 %collective-permute-start.13 = (bf16[384,512]{1,0:T(8,128)(2,1)S(1)}, bf16[384,512]{1,0:T(8,128)(2,1)}, u32[]{:S(2)}, u32[]{:S(2)}) collective-permute-start(bf16[384,512]{1,0:T(8,128)(2,1)S(1)} %slice.91), channel_id=1, source_target_pairs={{0,12},{1,13},{2,14},{3,15},{4,0},{5,1},{6,2},{7,3},{8,4},{9,5},{1... | collective-permute-start | bytes 1179656 | tf_op jit(solution)/shard_map/ppermute | solution.py:68
  155.1 16.1 %collective-permute-start.17 = (bf16[384,512]{1,0:T(8,128)(2,1)S(1)}, bf16[384,512]{1,0:T(8,128)(2,1)}, u32[]{:S(2)}, u32[]{:S(2)}) collective-permute-start(bf16[384,512]{1,0:T(8,128)(2,1)S(1)} %slice.92), channel_id=1, source_target_pairs={{0,4},{1,5},{2,6},{3,7},{4,8},{5,9},{6,10},{7,11},{8,12},{9,13},{1... | collective-permute-start | bytes 1179656 | tf_op jit(solution)/shard_map/ppermute | solution.py:67
  160.3 10.9 %collective-permute-start.18 = (bf16[384,512]{1,0:T(8,128)(2,1)S(1)}, bf16[384,512]{1,0:T(8,128)(2,1)}, u32[]{:S(2)}, u32[]{:S(2)}) collective-permute-start(bf16[384,512]{1,0:T(8,128)(2,1)S(1)} %slice.93), channel_id=1, source_target_pairs={{0,12},{1,13},{2,14},{3,15},{4,0},{5,1},{6,2},{7,3},{8,4},{9,5},{1... | collective-permute-start | bytes 1179656 | tf_op jit(solution)/shard_map/ppermute | solution.py:68
  171.2 0.8 copy-start.2
  171.9 23.1 %copy-start.12 = (s32[192]{0:T(256)S(1)}, s32[192]{0:T(256)}, u32[]{:S(2)}) copy-start(s32[192]{0:T(256)} %param.10) | copy-start | bytes 2308
  171.9 36.7 %copy-start = (bf16[768,1024]{1,0:T(8,128)(2,1)S(1)}, bf16[768,1024]{1,0:T(8,128)(2,1)}, u32[]{:S(2)}) copy-start(bf16[768,1024]{1,0:T(8,128)(2,1)} %student_ref.3) | copy-start | bytes 4718596
  194.9 4.1 %collective-permute-start.20 = (f32[8,768]{1,0:T(8,128)}, f32[8,768]{1,0:T(8,128)S(1)}, u32[]{:S(2)}, u32[]{:S(2)}) collective-permute-start(f32[8,768]{1,0:T(8,128)} %get-tuple-element.10), channel_id=1, source_target_pairs={{0,1},{1,0},{2,3},{3,2},{4,5},{5,4},{6,7},{7,6},{8,9},{9,8},{10,11... | collective-permute-start | bytes 73736 | tf_op jit(solution)/shard_map/ppermute | solution.py:224
  202.0 11.2 %collective-permute-start.21 = (f32[1,2]{1,0:T(1,128)S(1)}, f32[1,2]{1,0:T(1,128)S(1)}, u32[]{:S(2)}, u32[]{:S(2)}) collective-permute-start(f32[1,2]{1,0:T(1,128)S(1)} %maximum_bitcast_fusion), channel_id=1, source_target_pairs={{0,16},{16,0},{32,48},{48,32},{64,80},{80,64},{96,112},{112,96},{1... | collective-permute-start | bytes 32 | tf_op jit(solution)/shard_map/ppermute | solution.py:203
  202.0 11.2 %collective-permute-start.22 = (f32[1,2]{1,0:T(1,128)S(1)}, f32[1,2]{1,0:T(1,128)S(1)}, u32[]{:S(2)}, u32[]{:S(2)}) collective-permute-start(f32[1,2]{1,0:T(1,128)S(1)} %maximum_bitcast_fusion), channel_id=1, source_target_pairs={{0,128},{16,144},{32,160},{48,176},{64,192},{80,208},{96,224},{112... | collective-permute-start | bytes 32 | tf_op jit(solution)/shard_map/ppermute | solution.py:203
  206.6 6.9 %collective-permute-start.23 = (f32[1,2]{1,0:T(1,128)S(1)}, f32[1,2]{1,0:T(1,128)S(1)}, u32[]{:S(2)}, u32[]{:S(2)}) collective-permute-start(f32[1,2]{1,0:T(1,128)S(1)} %maximum_bitcast_fusion), channel_id=1, source_target_pairs={{0,144},{16,128},{32,176},{48,160},{64,208},{80,192},{96,240},{112... | collective-permute-start | bytes 32 | tf_op jit(solution)/shard_map/ppermute | solution.py:203
  208.7 1.9 copy-start.1
  214.8 5.4 %collective-permute-start.24 = (f32[1,2]{1,0:T(1,128)S(1)}, f32[1,2]{1,0:T(1,128)S(1)}, u32[]{:S(2)}, u32[]{:S(2)}) collective-permute-start(f32[1,2]{1,0:T(1,128)S(1)} %add_add_fusion.4), channel_id=1, source_target_pairs={{0,1},{1,2},{2,3},{3,0},{4,5},{5,6},{6,7},{7,4},{8,9},{9,10},{10,1... | collective-permute-start | bytes 32 | tf_op jit(solution)/shard_map/ppermute | solution.py:203
  214.8 5.3 %collective-permute-start.25 = (f32[1,2]{1,0:T(1,128)S(1)}, f32[1,2]{1,0:T(1,128)S(1)}, u32[]{:S(2)}, u32[]{:S(2)}) collective-permute-start(f32[1,2]{1,0:T(1,128)S(1)} %add_add_fusion.4), channel_id=1, source_target_pairs={{0,2},{1,3},{2,0},{3,1},{4,6},{5,7},{6,4},{7,5},{8,10},{9,11},{10,... | collective-permute-start | bytes 32 | tf_op jit(solution)/shard_map/ppermute | solution.py:203
  216.8 3.9 %collective-permute-start.26 = (f32[1,2]{1,0:T(1,128)S(1)}, f32[1,2]{1,0:T(1,128)S(1)}, u32[]{:S(2)}, u32[]{:S(2)}) collective-permute-start(f32[1,2]{1,0:T(1,128)S(1)} %add_add_fusion.4), channel_id=1, source_target_pairs={{0,3},{1,0},{2,1},{3,2},{4,7},{5,4},{6,5},{7,6},{8,11},{9,8},{10,9... | collective-permute-start | bytes 32 | tf_op jit(solution)/shard_map/ppermute | solution.py:203
  220.7 5.8 %collective-permute-start.27 = (f32[1,2]{1,0:T(1,128)S(1)}, f32[1,2]{1,0:T(1,128)S(1)}, u32[]{:S(2)}, u32[]{:S(2)}) collective-permute-start(f32[1,2]{1,0:T(1,128)S(1)} %add_add_fusion.3), channel_id=1, source_target_pairs={{0,32},{16,48},{32,64},{48,80},{64,96},{80,112},{96,0},{112,16},{1... | collective-permute-start | bytes 32 | tf_op jit(solution)/shard_map/ppermute | solution.py:203
  222.3 5.0 %collective-permute-start.28 = (f32[1,2]{1,0:T(1,128)S(1)}, f32[1,2]{1,0:T(1,128)S(1)}, u32[]{:S(2)}, u32[]{:S(2)}) collective-permute-start(f32[1,2]{1,0:T(1,128)S(1)} %add_add_fusion.3), channel_id=1, source_target_pairs={{0,64},{16,80},{32,96},{48,112},{64,0},{80,16},{96,32},{112,48},{1... | collective-permute-start | bytes 32 | tf_op jit(solution)/shard_map/ppermute | solution.py:203
  225.2 3.5 %collective-permute-start.29 = (f32[1,2]{1,0:T(1,128)S(1)}, f32[1,2]{1,0:T(1,128)S(1)}, u32[]{:S(2)}, u32[]{:S(2)}) collective-permute-start(f32[1,2]{1,0:T(1,128)S(1)} %add_add_fusion.3), channel_id=1, source_target_pairs={{0,96},{16,112},{32,0},{48,16},{64,32},{80,48},{96,64},{112,80},{1... | collective-permute-start | bytes 32 | tf_op jit(solution)/shard_map/ppermute | solution.py:203
  228.7 7.7 %collective-permute-start.30 = (f32[1,2]{1,0:T(1,128)S(1)}, f32[1,2]{1,0:T(1,128)S(1)}, u32[]{:S(2)}, u32[]{:S(2)}) collective-permute-start(f32[1,2]{1,0:T(1,128)S(1)} %add_add_fusion.2), channel_id=1, source_target_pairs={{0,4},{1,5},{2,6},{3,7},{4,8},{5,9},{6,10},{7,11},{8,12},{9,13},{1... | collective-permute-start | bytes 32 | tf_op jit(solution)/shard_map/ppermute | solution.py:203
  231.1 5.3 %collective-permute-start.31 = (f32[1,2]{1,0:T(1,128)S(1)}, f32[1,2]{1,0:T(1,128)S(1)}, u32[]{:S(2)}, u32[]{:S(2)}) collective-permute-start(f32[1,2]{1,0:T(1,128)S(1)} %add_add_fusion.2), channel_id=1, source_target_pairs={{0,8},{1,9},{2,10},{3,11},{4,12},{5,13},{6,14},{7,15},{8,0},{9,1},... | collective-permute-start | bytes 32 | tf_op jit(solution)/shard_map/ppermute | solution.py:203
  234.1 3.6 %collective-permute-start.32 = (f32[1,2]{1,0:T(1,128)S(1)}, f32[1,2]{1,0:T(1,128)S(1)}, u32[]{:S(2)}, u32[]{:S(2)}) collective-permute-start(f32[1,2]{1,0:T(1,128)S(1)} %add_add_fusion.2), channel_id=1, source_target_pairs={{0,12},{1,13},{2,14},{3,15},{4,0},{5,1},{6,2},{7,3},{8,4},{9,5},{1... | collective-permute-start | bytes 32 | tf_op jit(solution)/shard_map/ppermute | solution.py:203
Sparse Core Ops, SparseCore 0:
  9.9 55.2 all-gather.4
  67.6 52.4 all-gather.6

commit v2 on v1

v2 whole, which is shorter than its diff:
```python
import functools

import jax
import jax.numpy as jnp
from jax import lax
from jax.experimental import pallas as pl
from jax.experimental.pallas import tpu as pltpu
from jax.sharding import PartitionSpec as P

V = 2048
CB = 8
STEPS = 4
NX = 4
NZ = 4
NY = 4
NH = 2
BLOCKS = 16
CHUNK = 128
MIB = 1 << 20


def tp_at(x, z):
    return x * NZ + z


def row_at(h, y, c):
    return h * 2 * NY + y * 2 + c


def x_ring(d):
    return [(tp_at(x, z), tp_at((x + d) % NX, z)) for x in range(NX) for z in range(NZ)]


def z_ring(d):
    return [(tp_at(x, z), tp_at(x, (z + d) % NZ)) for x in range(NX) for z in range(NZ)]


def y_ring(d):
    return [
        (row_at(h, y, c), row_at(h, (y + d) % NY, c))
        for h in range(NH)
        for y in range(NY)
        for c in range(2)
    ]


def z_whole(d):
    at = [(h, z) for h in range(NH) for z in range(NZ)]
    moves = [(one, at[(i + d) % len(at)]) for i, one in enumerate(at)]
    return [
        (row_at(h, y, c) * BLOCKS + tp_at(x, z), row_at(h2, y, c) * BLOCKS + tp_at(x, z2))
        for (h, z), (h2, z2) in moves
        for y in range(NY)
        for c in range(2)
        for x in range(NX)
    ]


def row_xor(m):
    return [(r, r ^ m) for r in range(16)]


PAIR = [(t, t ^ 1) for t in range(16)]
SAME_HALF = [[row_at(h, y, c) for y in range(NY) for c in range(2)] for h in range(NH)]


def after(value, *earlier):
    return lax.optimization_barrier((value,) + earlier)[0]


def teacher_logits(weight, own, accumulate):
    half = own.shape[0] // 2
    cut = weight.shape[0] // 2

    def x_hop(value, d):
        return lax.ppermute(value, "tp", x_ring(d))

    def z_hop(value):
        return lax.ppermute(value, "tp", z_ring(1))

    def widen(shard):
        return lax.all_gather(shard, "rows", axis_index_groups=SAME_HALF)

    def far_hop(value, d):
        return lax.ppermute(value, ("rows", "tp"), z_whole(d))

    near = widen(weight)
    z1 = z_hop(own)
    left0, right0 = x_hop(own, 1), x_hop(own, -1)
    up, down = far_hop(weight[:cut], 2), far_hop(weight[cut:], -2)
    top0, low0 = x_hop(left0[:half], 1), x_hop(right0[half:], -1)

    here1, up, down, *_ = lax.optimization_barrier((z1, up, down, top0, low0))
    left1, right1 = x_hop(here1, 1), x_hop(here1, -1)
    up, down = far_hop(up, 2), far_hop(down, -2)
    up, down, here1, to_right, to_left = lax.optimization_barrier(
        (up, down, here1, left1, right1)
    )
    far = widen(jnp.concatenate([up, down]))
    z2 = z_hop(here1)
    top1, low1 = x_hop(to_right[:half], 1), x_hop(to_left[half:], -1)

    here2, *_ = lax.optimization_barrier((z2, top1, low1))
    z3 = z_hop(here2)
    left2, right2 = x_hop(here2, 1), x_hop(here2, -1)

    here3, to_right, to_left = lax.optimization_barrier((z3, left2, right2))
    left3, right3 = x_hop(here3, 1), x_hop(here3, -1)
    top2, low2 = x_hop(to_right[:half], 1), x_hop(to_left[half:], -1)
    blocks = [(own,), (left0,), (top0, low0), (right0,)]
    blocks += [(z1,), (left1,), (top1, low1), (right1,)]
    state = accumulate(0, blocks, near, far)

    to_right, to_left, *_ = lax.optimization_barrier((left3, right3, top2, low2, *state))
    top3, low3 = x_hop(to_right[:half], 1), x_hop(to_left[half:], -1)
    blocks = [(z2,), (left2,), (top2, low2), (right2,), (z3,), (left3,), (right3,)]
    state = accumulate(8, blocks, near, far, state)
    return accumulate(15, [(top3, low3)], near, far, state)


def start_block(block, to, sem):
    at = 0
    for part in block:
        rows = part.shape[0]
        pltpu.make_async_copy(part, to.at[pl.ds(at, rows)], sem).start()
        at += rows


def teacher_kernel(first, shape, plan_ref, gain_ref, near_ref, far_ref, *refs):
    refs = list(refs)
    count = len(shape)
    last = first + count == BLOCKS
    student_ref = refs.pop(0) if last else None
    start_refs = [refs.pop(0), refs.pop(0)] if first else []
    blocks = [[refs.pop(0) for _ in range(parts)] for parts in shape]
    teach_ref, side_ref, a_vm, w_vm, a_sem, w_sem, start_sem, *square_ref = refs
    square_ref = square_ref[0] if last else side_ref
    tok = teach_ref.shape[0]
    starts = [
        pltpu.make_async_copy(ref, to, start_sem.at[at])
        for at, (ref, to) in enumerate(zip(start_refs, (teach_ref, square_ref)))
    ]
    for step in range(count):
        start_block(blocks[step], a_vm.at[step], a_sem.at[step])
        slot = plan_ref[first + step]

        @pl.when(slot < 8)
        def _():
            pltpu.make_async_copy(near_ref.at[slot], w_vm.at[step], w_sem.at[step]).start()

        @pl.when(slot >= 8)
        def _():
            pltpu.make_async_copy(far_ref.at[slot - 8], w_vm.at[step], w_sem.at[step]).start()

        if step == 0:
            for copy in starts:
                copy.start()
    if first:
        for copy in starts:
            copy.wait()
    else:
        square_ref[...] = jnp.zeros_like(square_ref)
        teach_ref[...] = jnp.zeros_like(teach_ref)

    def step_body(step, carry):
        pltpu.make_async_copy(a_vm.at[step], a_vm.at[step], a_sem.at[step]).wait()
        pltpu.make_async_copy(w_vm.at[step], w_vm.at[step], w_sem.at[step]).wait()
        gain = gain_ref[plan_ref[BLOCKS + first + step]]
        for r in range(0, tok, 256):
            wide = a_vm[step, r : r + 256, :].astype(jnp.float32)
            square = wide * wide
            square_ref[r : r + 256, :] += (
                square[:, :128] + square[:, 128:256] + square[:, 256:384] + square[:, 384:]
            )
            normed = (wide * gain).astype(jnp.bfloat16)
            teach_ref[r : r + 256, :] += jnp.dot(
                normed, w_vm[step], preferred_element_type=jnp.float32
            )
        return carry

    lax.fori_loop(0, count, step_body, 0)
    if last:
        statistics(teach_ref, square_ref, student_ref, side_ref)


def statistics(teach_ref, square_ref, student_ref, stats_ref):
    lane = lax.broadcasted_iota(jnp.int32, (CHUNK, 128), 1)
    for r in range(0, teach_ref.shape[0], CHUNK):
        rows = pl.ds(r, CHUNK)
        mean = jnp.sum(square_ref[rows, :], axis=1, keepdims=True) / (BLOCKS * 512)
        teach = teach_ref[rows, :] * lax.rsqrt(mean + 1e-05)
        teach_ref[rows, :] = teach
        stud = student_ref[rows, :].astype(jnp.float32)
        teach_peak = jnp.max(teach, axis=1, keepdims=True)
        stud_peak = jnp.max(stud, axis=1, keepdims=True)
        teach = teach - teach_peak
        stud = stud - stud_peak
        mass = jnp.exp(stud)
        teach_total = jnp.sum(jnp.exp(teach), axis=1, keepdims=True)
        stud_total = jnp.sum(mass, axis=1, keepdims=True)
        cross = jnp.sum(mass * (stud - teach), axis=1, keepdims=True)
        packed = jnp.zeros((CHUNK, 128), jnp.float32)
        for at, value in enumerate((teach_peak, teach_total, stud_peak, stud_total, cross)):
            packed = jnp.where(lane == at, value, packed)
        stats_ref[:, r : r + CHUNK] = packed.T[:8, :]


def accumulate_blocks(gain, student, plan, first, blocks, near, far, state=()):
    tok, cols = student.shape
    hbm = pl.BlockSpec(memory_space=pltpu.HBM)
    vmem = pl.BlockSpec(memory_space=pltpu.VMEM)
    smem = pl.BlockSpec(memory_space=pltpu.SMEM)
    logits = jax.ShapeDtypeStruct((tok, cols), jnp.float32)
    squares = jax.ShapeDtypeStruct((tok, 128), jnp.float32)
    stats = jax.ShapeDtypeStruct((8, tok), jnp.float32)
    count = len(blocks)
    last = first + count == BLOCKS
    parts = [part for block in blocks for part in block]
    scratch = [
        pltpu.VMEM((count, tok, 512), jnp.bfloat16),
        pltpu.VMEM((count, 512, cols), jnp.bfloat16),
        pltpu.SemaphoreType.DMA((count,)),
        pltpu.SemaphoreType.DMA((count,)),
        pltpu.SemaphoreType.DMA((2,)),
    ]
    return pl.pallas_call(
        functools.partial(teacher_kernel, first, [len(block) for block in blocks]),
        out_shape=(logits, stats if last else squares),
        in_specs=[smem, vmem, hbm, hbm] + [vmem] * last + [hbm] * (len(state) + len(parts)),
        out_specs=(vmem, vmem),
        scratch_shapes=scratch + [pltpu.VMEM((tok, 128), jnp.float32)] * last,
        compiler_params=pltpu.CompilerParams(vmem_limit_bytes=60 * MIB),
        name="teacher_" + str(first),
    )(plan, gain.reshape(BLOCKS, 1, 512), near, far, *([student] * last), *state, *parts)


def block_plan():
    tp = lax.axis_index("tp")
    half = lax.axis_index("rows") // 8
    x, z = tp // NZ, tp % NZ
    blocks = []
    for i in range(NZ):
        for off in (0, 1, 2, 3) if i < 3 else (0, 1, 3, 2):
            blocks.append(((x - off) % NX) * NZ + (z - i) % NZ)
    slots = [jnp.where(k // 8 == half, k % 8, 8 + k % 8) for k in blocks]
    return jnp.stack(slots + blocks).astype(jnp.int32)


def combine_kernel(own_ref, other_ref, live_ref, count_ref, coef_ref, sums_ref):
    own = [own_ref[at : at + 1, :] for at in range(5)]
    other = [other_ref[at : at + 1, :] for at in range(5)]
    live = live_ref[...]
    teach_peak = jnp.maximum(own[0], other[0])
    stud_peak = jnp.maximum(own[2], other[2])
    teach_total = stud_total = cross = 0.0
    for part in (own, other):
        teach_low = part[0] - teach_peak
        stud_low = part[2] - stud_peak
        weight = jnp.exp(stud_low)
        teach_total = teach_total + jnp.exp(teach_low) * part[1]
        stud_total = stud_total + weight * part[3]
        cross = cross + weight * (part[4] + part[3] * (stud_low - teach_low))
    log_stud = jnp.log(stud_total)
    log_teach = jnp.log(teach_total)
    divergence = cross / stud_total - (log_stud - log_teach)
    coef_ref[...] = jnp.zeros_like(coef_ref)
    coef_ref[0:1, :] = stud_peak
    coef_ref[1:2, :] = log_stud
    coef_ref[2:3, :] = (stud_peak - teach_peak) + (log_stud - log_teach) + divergence
    coef_ref[3:4, :] = V * live
    lane = lax.broadcasted_iota(jnp.int32, (1, 128), 1)
    total = jnp.sum(live * divergence, axis=1, keepdims=True)
    sums_ref[...] = jnp.where(lane == 0, total, jnp.where(lane == 1, count_ref[0], 0.0))


def combine(own, other, live, count):
    vmem = pl.BlockSpec(memory_space=pltpu.VMEM)
    return pl.pallas_call(
        combine_kernel,
        out_shape=(
            jax.ShapeDtypeStruct(own.shape, jnp.float32),
            jax.ShapeDtypeStruct((1, 128), jnp.float32),
        ),
        in_specs=[vmem, vmem, vmem, pl.BlockSpec(memory_space=pltpu.SMEM)],
        out_specs=(vmem, vmem),
        name="combine",
    )(own, other, live, count)


def grad_kernel(coef_ref, teach_ref, student_ref, grad_ref):
    coef = coef_ref[...].T
    stud = student_ref[...].astype(jnp.float32)
    prob = jnp.exp((stud - coef[:, 0:1]) - coef[:, 1:2])
    differ = (stud - teach_ref[...]) - coef[:, 2:3]
    grad_ref[...] = ((coef[:, 3:4] * prob) * differ).astype(jnp.bfloat16)


def gradient(coef, teach, student):
    tok, cols = student.shape
    tile = 256
    return pl.pallas_call(
        grad_kernel,
        grid=(tok // tile,),
        out_shape=jax.ShapeDtypeStruct((tok, cols), jnp.bfloat16),
        in_specs=[
            pl.BlockSpec((8, tile), lambda i: (0, i)),
            pl.BlockSpec((tile, cols), lambda i: (i, 0)),
            pl.BlockSpec((tile, cols), lambda i: (i, 0)),
        ],
        out_specs=pl.BlockSpec((tile, cols), lambda i: (i, 0)),
        compiler_params=pltpu.CompilerParams(vmem_limit_bytes=60 * MIB),
        name="gradient",
    )(coef, teach, student)


def total_everywhere(value):
    for axis, moves in (
        ("tp", [[(t, t ^ 2) for t in range(BLOCKS)]]),
        ("rows", [row_xor(m) for m in (1, 8, 9)]),
        ("rows", [y_ring(d) for d in (1, 2, 3)]),
        ("tp", [x_ring(d) for d in (1, 2, 3)]),
    ):
        value = sum([lax.ppermute(value, axis, move) for move in moves], value)
    return value


def body(teacher_hidden, norm_gain, head_weight, student_logits, row_lengths):
    tok = teacher_hidden.shape[0]
    steps_of = jnp.arange(tok, dtype=jnp.int32) % STEPS
    live = (steps_of < jnp.repeat(row_lengths, STEPS)).astype(jnp.float32)
    count = jnp.sum(row_lengths.astype(jnp.float32))
    accumulate = functools.partial(accumulate_blocks, norm_gain, student_logits, block_plan())
    teach, stats = teacher_logits(head_weight, teacher_hidden, accumulate)
    other = lax.ppermute(stats, "tp", PAIR)
    coef, sums = combine(stats, other, live.reshape(1, tok), count.reshape(1))
    grad = gradient(coef, teach, student_logits)
    sums = total_everywhere(sums)
    loss = sums[0, 0] / (CB * (sums[0, 1] / (BLOCKS // 2)))
    return (grad, loss)


def solution(mesh):
    in_specs = (P("rows", "tp"), P(), P("rows", "tp"), P("rows", "tp"), P("rows"))
    out_specs = (P("rows", "tp"), P())
    return jax.shard_map(body, mesh=mesh, in_specs=in_specs, out_specs=out_specs, check_vma=False)
```

time: 250 us -> 233 us (0.932)
  Pallas kernels: 25.7 us -> 41.8 us
  waiting for transfers between devices: 130 us -> 114 us
  starting transfers between devices: 59 us -> 50.4 us
  other arithmetic: 6.44 us -> 3 us
  local copies, waits for them, and re-layouts: 9.95 us -> 6.63 us
    ppermute x32 -> x33, waiting for transfers between devices: 127 us -> 107 us  [the longest x4 47.9 us: far_hop(): return lax.ppermute(value, ('rows', 'tp'), z_whole(d))]
    pallas_call x1 -> x4, Pallas kernels: 23 us -> 36.8 us  [the longest x3 34.7 us: accumulate_blocks(): pl.pallas_call(functools.partial(teacher_kernel, first, [len(block) for b...]
    ppermute x32 -> x33, starting transfers between devices: 58.9 us -> 50.2 us  [the longest x16 20.1 us: x_hop(): return lax.ppermute(value, 'tp', x_ring(d))]
    all_gather x2, waiting for transfers between devices: 0.01 us -> 2.57 us  [widen(): return lax.all_gather(shard, 'rows', axis_index_groups=SAME_HALF)]
    slice x9 -> x10, local copies, waits for them, and re-layouts: 5.04 us -> 4.19 us  [the longest x2 2.19 us: teacher_logits(): top3, low3 = (x_hop(to_right[:half], 1), x_hop(to_left[half:], -1))]
  transfers between devices with their start and end apart: 35 -> 36, of which waited for: 21 -> 17; matrix products, arithmetic and copies ran while one was open for 3% -> 2% of each run, Pallas kernels for 1% -> 14%
where the time goes in v2:
time: 233 us
  waiting for transfers between devices  114 us (49%)
  starting transfers between devices  50.4 us (22%)
  Pallas kernels  41.8 us (18%)
  between operations  17.4 us (7%)
  local copies, waits for them, and re-layouts  6.63 us (3%)
  other arithmetic  3 us (1%)
    ppermute x4, waiting for transfers between devices, far_hop(): return lax.ppermute(value, ('rows', 'tp'), z_whole(d))  47.9 us
    ppermute x16, waiting for transfers between devices, x_hop(): return lax.ppermute(value, 'tp', x_ring(d))  39.6 us
    pallas_call x3, Pallas kernels, accumulate_blocks(): pl.pallas_call(functools.partial(teacher_kernel, first, [len(block) for b...  34.7 us
    ppermute x16, starting transfers between devices, x_hop(): return lax.ppermute(value, 'tp', x_ring(d))  20.1 us
    ppermute x10, starting transfers between devices, total_everywhere(): value = sum([lax.ppermute(value, axis, move) for move in moves], value)  17.5 us
    ppermute x3, waiting for transfers between devices, z_hop(): return lax.ppermute(value, 'tp', z_ring(1))  10.5 us
    ppermute x4, starting transfers between devices, far_hop(): return lax.ppermute(value, ('rows', 'tp'), z_whole(d))  9.7 us
    ppermute x10, waiting for transfers between devices, total_everywhere(): value = sum([lax.ppermute(value, axis, move) for move in moves], value)  8.96 us
  transfers between devices with their start and end apart: 36, of which 17 were waited for; matrix products, arithmetic and copies ran while one was open for 2% of the time, Pallas kernels for 14%

profile of v2, /device:TPU:2, one launch (start us, length us, event | category | flops | bytes accessed | tf_op | source)
XLA Modules:
  0.0 232.7 jit_solution(9533355588114393799)
XLA Ops:
  7.2 0.7 all-gather.5.cloned.1.call-update
  7.9 1.6 collective-permute-start.3
  9.5 0.9 collective-permute-start.5
  10.4 1.6 collective-permute-start
  12.0 1.3 fusion
  13.2 3.3 %collective-permute-start.1 = (bf16[256,1024]{1,0:T(8,128)(2,1)S(1)}, bf16[256,1024]{1,0:T(8,128)(2,1)S(1)}, u32[]{:S(2)}, u32[]{:S(2)}) collective-permute-start(bf16[256,1024]{1,0:T(8,128)(2,1)S(1)} %get-tuple-element.47), channel_id=1, source_target_pairs={{0,2},{4,6},{8,10},{12,14},{16,18},{20,22},{24,26},{28,30},{32,34}... | collective-permute-start | bytes 1572872 | tf_op jit(solution)/shard_map/ppermute | solution.py:85
  16.6 2.2 collective-permute-start.2
  18.8 8.7 %collective-permute-done.3.refs_1_ = bf16[768,512]{1,0:T(8,128)(2,1)S(1)} collective-permute-done((bf16[768,512]{1,0:T(8,128)(2,1)}, bf16[768,512]{1,0:T(8,128)(2,1)S(1)}, u32[]{:S(2)}, u32[]{:S(2)}) %collective-permute-start.3) | collective-permute-done | bytes 786464 | tf_op jit(solution)/shard_map/ppermute | solution.py:76
  27.5 1.6 collective-permute-start.4
  29.1 0.6 collective-permute-start.6
  29.8 27.0 %collective-permute-done.1 = bf16[256,1024]{1,0:T(8,128)(2,1)S(1)} collective-permute-done((bf16[256,1024]{1,0:T(8,128)(2,1)S(1)}, bf16[256,1024]{1,0:T(8,128)(2,1)S(1)}, u32[]{:S(2)}, u32[]{:S(2)}) %collective-permute-start.1) | collective-permute-done | bytes 524320 | tf_op jit(solution)/shard_map/ppermute | solution.py:85
  56.8 1.6 collective-permute-start.9
  58.4 0.5 collective-permute-start.10
  58.9 4.1 %collective-permute-start.8 = (bf16[256,1024]{1,0:T(8,128)(2,1)S(1)}, bf16[256,1024]{1,0:T(8,128)(2,1)S(1)}, u32[]{:S(2)}, u32[]{:S(2)}) collective-permute-start(bf16[256,1024]{1,0:T(8,128)(2,1)S(1)} %collective-permute-done.2), channel_id=1, source_target_pairs={{0,130},{4,134},{8,138},{12,142},{16,146},{20,150},{24,154},{28,15... | collective-permute-start | bytes 1572872 | tf_op jit(solution)/shard_map/ppermute | solution.py:85
  63.0 20.9 %collective-permute-done.7 = bf16[256,1024]{1,0:T(8,128)(2,1)S(1)} collective-permute-done((bf16[256,1024]{1,0:T(8,128)(2,1)S(1)}, bf16[256,1024]{1,0:T(8,128)(2,1)S(1)}, u32[]{:S(2)}, u32[]{:S(2)}) %collective-permute-start.7) | collective-permute-done | bytes 524320 | tf_op jit(solution)/shard_map/ppermute | solution.py:85
  84.0 1.2 pad_maximum_fusion
  85.2 1.4 collective-permute-start.13
  86.6 1.5 collective-permute-start.11
  88.1 1.6 collective-permute-start.12
  89.7 8.3 %collective-permute-done.11.refs_7_ = bf16[384,512]{1,0:T(8,128)(2,1)S(1)} collective-permute-done((bf16[384,512]{1,0:T(8,128)(2,1)S(1)}, bf16[384,512]{1,0:T(8,128)(2,1)S(1)}, u32[]{:S(2)}, u32[]{:S(2)}) %collective-permute-start.11) | collective-permute-done | bytes 393248 | tf_op jit(solution)/shard_map/ppermute | solution.py:76
  98.1 8.6 %collective-permute-done.13.refs_2_ = bf16[768,512]{1,0:T(8,128)(2,1)S(1)} collective-permute-done((bf16[768,512]{1,0:T(8,128)(2,1)}, bf16[768,512]{1,0:T(8,128)(2,1)S(1)}, u32[]{:S(2)}, u32[]{:S(2)}) %collective-permute-start.13) | collective-permute-done | bytes 786464 | tf_op jit(solution)/shard_map/ppermute | solution.py:79
  106.6 1.4 collective-permute-start.14
  108.0 1.6 collective-permute-start.16
  109.6 16.5 %collective-permute-done.14.refs_3_ = bf16[768,512]{1,0:T(8,128)(2,1)S(1)} collective-permute-done((bf16[768,512]{1,0:T(8,128)(2,1)S(1)}, bf16[768,512]{1,0:T(8,128)(2,1)S(1)}, u32[]{:S(2)}, u32[]{:S(2)}) %collective-permute-start.14) | collective-permute-done | bytes 786464 | tf_op jit(solution)/shard_map/ppermute | solution.py:76
  126.1 1.9 collective-permute-done.15.refs_7_
  128.0 1.2 collective-permute-start.19
  129.2 0.8 collective-permute-start.20
  130.1 2.2 collective-permute-start.17
  132.3 1.0 collective-permute-start.18
  133.9 0.7 stack.131.plan_ref
  134.6 2.6 %all-gather.7.cloned.1.call-done = bf16[4096,1024]{1,0:T(8,128)(2,1)} async-done(((bf16[512,1024]{1,0:T(8,128)(2,1)}), bf16[4096,1024]{1,0:T(8,128)(2,1)}) %all-gather.7.cloned.1.call-update) | async-done | bytes 8388624 | tf_op jit(solution)/shard_map/all_gather | solution.py:82
  137.2 12.7 %teacher_0.1 = (f32[768,1024]{1,0:T(8,128)}, f32[768,128]{1,0:T(8,128)}) custom-call(s32[32]{0:T(128)} %stack.131.plan_ref, f32[16,1,512]{2,1,0:T(1,128)} %bitcast.43, bf16[8,512,1024]{2,1,0:T(8,128)(2,1)} %bitcast.37, bf16[8,512,1024]{2,1,0:T(8,128)(2,1)} %bitcast.40, bf16[768,512]{1,0:T(8,128)(2,1)} %refs_0_.2, bf16[768,512]{1,0:T(8,128)(2,1)} %copy-done, ...), custom_call_target="tpu_custom_call" | custom-call | tf_op jit(solution)/shard_map/teacher_0/pallas_call | solution.py:226
  149.9 4.3 %collective-permute-done.17.refs_4_ = bf16[384,512]{1,0:T(8,128)(2,1)} collective-permute-done((bf16[384,512]{1,0:T(8,128)(2,1)S(1)}, bf16[384,512]{1,0:T(8,128)(2,1)}, u32[]{:S(2)}, u32[]{:S(2)}) %collective-permute-start.17) | collective-permute-done | bytes 393248 | tf_op jit(solution)/shard_map/ppermute | solution.py:76
  154.2 1.7 collective-permute-done.18.refs_5_
  155.9 1.2 slice.44
  157.0 1.8 collective-permute-start.21
  158.8 1.0 slice.45
  159.9 0.4 collective-permute-start.22
  160.3 0.1 reshape.53
  160.5 0.6 compare_convert_fusion.live_ref
  161.1 14.7 %teacher_8.1 = (f32[768,1024]{1,0:T(8,128)}, f32[768,128]{1,0:T(8,128)}) custom-call(s32[32]{0:T(128)} %stack.131.plan_ref, f32[16,1,512]{2,1,0:T(1,128)} %bitcast.44, bf16[8,512,1024]{2,1,0:T(8,128)(2,1)} %bitcast.38, bf16[8,512,1024]{2,1,0:T(8,128)(2,1)} %bitcast.41, f32[768,1024]{1,0:T(8,128)} %get-tuple-element.31.refs_0_, ...), custom_call_target="tpu_custom_call" | custom-call | tf_op jit(solution)/shard_map/teacher_8/pallas_call | solution.py:226
  175.8 0.7 copy-done.13
  176.5 0.2 copy-done.14
  176.7 7.4 %teacher_15.1 = (f32[768,1024]{1,0:T(8,128)}, f32[8,768]{1,0:T(8,128)}) custom-call(s32[32]{0:T(128)} %stack.131.plan_ref, f32[16,1,512]{2,1,0:T(1,128)} %bitcast.45, bf16[8,512,1024]{2,1,0:T(8,128)(2,1)} %bitcast.39, bf16[8,512,1024]{2,1,0:T(8,128)(2,1)} %bitcast.42, bf16[768,1024]{1,0:T(8,128)(2,1)} %student_ref.1, f32[768,1024]{1,0:T(8,128)} %get-tuple-element.38.refs_1_, ...), custom_call_target="tpu_custom_call" | custom-call | tf_op jit(solution)/shard_map/teacher_15/pallas_call | solution.py:226
  184.1 0.6 convert_reduce_fusion
  184.7 3.4 %collective-permute-done.23.other_ref = f32[8,768]{1,0:T(8,128)S(1)} collective-permute-done((f32[8,768]{1,0:T(8,128)}, f32[8,768]{1,0:T(8,128)S(1)}, u32[]{:S(2)}, u32[]{:S(2)}) %collective-permute-start.23) | collective-permute-done | bytes 24608 | tf_op jit(solution)/shard_map/ppermute | solution.py:334
  188.2 0.6 copy-done.15
  188.8 2.0 combine.1
  190.8 1.2 collective-permute-start.24
  192.0 3.4 %collective-permute-done.24 = f32[1,128]{1,0:T(1,128)S(1)} collective-permute-done((f32[1,128]{1,0:T(1,128)}, f32[1,128]{1,0:T(1,128)S(1)}, u32[]{:S(2)}, u32[]{:S(2)}) %collective-permute-start.24) | collective-permute-done | bytes 544 | tf_op jit(solution)/shard_map/ppermute | solution.py:323
  195.5 0.6 add.337
  196.2 5.7 %collective-permute-start.25 = (f32[1,128]{1,0:T(1,128)S(1)}, f32[1,128]{1,0:T(1,128)S(1)}, u32[]{:S(2)}, u32[]{:S(2)}) collective-permute-start(f32[1,128]{1,0:T(1,128)S(1)} %add.337), channel_id=1, source_target_pairs={{0,16},{16,0},{32,48},{48,32},{64,80},{80,64},{96,112},{112,96},{1... | collective-permute-start | bytes 1544 | tf_op jit(solution)/shard_map/ppermute | solution.py:323
  201.9 1.1 collective-permute-done.27
  203.0 0.6 collective-permute-done.26
  203.6 3.1 %collective-permute-start.30 = (f32[1,128]{1,0:T(1,128)S(1)}, f32[1,128]{1,0:T(1,128)S(1)}, u32[]{:S(2)}, u32[]{:S(2)}) collective-permute-start(f32[1,128]{1,0:T(1,128)S(1)} %add_add_fusion.2), channel_id=1, source_target_pairs={{0,96},{16,112},{32,0},{48,16},{64,32},{80,48},{96,64},{112,80},{1... | collective-permute-start | bytes 1544 | tf_op jit(solution)/shard_map/ppermute | solution.py:323
  206.7 0.6 collective-permute-start.29
  207.3 0.9 collective-permute-start.28
  208.2 3.5 %collective-permute-done.29 = f32[1,128]{1,0:T(1,128)S(1)} collective-permute-done((f32[1,128]{1,0:T(1,128)S(1)}, f32[1,128]{1,0:T(1,128)S(1)}, u32[]{:S(2)}, u32[]{:S(2)}) %collective-permute-start.29) | collective-permute-done | bytes 544 | tf_op jit(solution)/shard_map/ppermute | solution.py:323
  211.7 0.3 collective-permute-done.28
  212.0 2.8 %collective-permute-start.33 = (f32[1,128]{1,0:T(1,128)S(1)}, f32[1,128]{1,0:T(1,128)S(1)}, u32[]{:S(2)}, u32[]{:S(2)}) collective-permute-start(f32[1,128]{1,0:T(1,128)S(1)} %add_add_fusion.1), channel_id=1, source_target_pairs={{0,12},{1,13},{2,14},{3,15},{4,0},{5,1},{6,2},{7,3},{8,4},{9,5},{1... | collective-permute-start | bytes 1544 | tf_op jit(solution)/shard_map/ppermute | solution.py:323
  214.8 0.6 collective-permute-start.32
  215.3 2.5 %collective-permute-start.31 = (f32[1,128]{1,0:T(1,128)S(1)}, f32[1,128]{1,0:T(1,128)S(1)}, u32[]{:S(2)}, u32[]{:S(2)}) collective-permute-start(f32[1,128]{1,0:T(1,128)S(1)} %add_add_fusion.1), channel_id=1, source_target_pairs={{0,4},{1,5},{2,6},{3,7},{4,8},{5,9},{6,10},{7,11},{8,12},{9,13},{1... | collective-permute-start | bytes 1544 | tf_op jit(solution)/shard_map/ppermute | solution.py:323
  217.9 5.0 %gradient.1 = bf16[768,1024]{1,0:T(8,128)(2,1)} custom-call(f32[8,768]{1,0:T(8,128)} %get-tuple-element.43.coef_ref, f32[768,1024]{1,0:T(8,128)} %get-tuple-element.44.teach_ref, bf16[768,1024]{1,0:T(8,128)(2,1)} %student_ref.1), custom_call_target="tpu_custom_call" | custom-call | tf_op jit(solution)/shard_map/gradient/pallas_call | solution.py:301
  222.9 0.6 fusion.1
  (69 shorter events, 0.8 us)
Async XLA Ops:
  7.2 127.5 %all-gather.5.cloned.1.call-start = ((), (), s32[]{:S(2)}) async-start(), calls=%async_computation | async-start | bytes 9437184 | tf_op jit(solution)/shard_map/all_gather | solution.py:82
  7.9 129.3 %all-gather.7.cloned.1.call-start = ((), (), s32[]{:S(2)}) async-start(), calls=%async_computation.1 | async-start | bytes 9437184 | tf_op jit(solution)/shard_map/all_gather | solution.py:82
  7.9 19.6 %collective-permute-start.3 = (bf16[768,512]{1,0:T(8,128)(2,1)}, bf16[768,512]{1,0:T(8,128)(2,1)S(1)}, u32[]{:S(2)}, u32[]{:S(2)}) collective-permute-start(bf16[768,512]{1,0:T(8,128)(2,1)} %refs_0_.2), channel_id=1, source_target_pairs={{0,4},{1,5},{2,6},{3,7},{4,8},{5,9},{6,10},{7,11},{8,12},{9,13},{1... | collective-permute-start | bytes 2359304 | tf_op jit(solution)/shard_map/ppermute | solution.py:76
  9.5 19.6 %collective-permute-start.5 = (bf16[768,512]{1,0:T(8,128)(2,1)}, bf16[768,512]{1,0:T(8,128)(2,1)S(1)}, u32[]{:S(2)}, u32[]{:S(2)}) collective-permute-start(bf16[768,512]{1,0:T(8,128)(2,1)} %refs_0_.2), channel_id=1, source_target_pairs={{0,12},{1,13},{2,14},{3,15},{4,0},{5,1},{6,2},{7,3},{8,4},{9,5},{1... | collective-permute-start | bytes 2359304 | tf_op jit(solution)/shard_map/ppermute | solution.py:76
  10.4 46.4 %collective-permute-start = (bf16[768,512]{1,0:T(8,128)(2,1)}, bf16[768,512]{1,0:T(8,128)(2,1)S(1)}, u32[]{:S(2)}, u32[]{:S(2)}) collective-permute-start(bf16[768,512]{1,0:T(8,128)(2,1)} %refs_0_.2), channel_id=1, source_target_pairs={{0,1},{1,2},{2,3},{3,0},{4,5},{5,6},{6,7},{7,4},{8,9},{9,10},{10,1... | collective-permute-start | bytes 2359304 | tf_op jit(solution)/shard_map/ppermute | solution.py:79
  13.2 43.5 %collective-permute-start.1 = (bf16[256,1024]{1,0:T(8,128)(2,1)S(1)}, bf16[256,1024]{1,0:T(8,128)(2,1)S(1)}, u32[]{:S(2)}, u32[]{:S(2)}) collective-permute-start(bf16[256,1024]{1,0:T(8,128)(2,1)S(1)} %get-tuple-element.47), channel_id=1, source_target_pairs={{0,2},{4,6},{8,10},{12,14},{16,18},{20,22},{24,26},{28,30},{32,34}... | collective-permute-start | bytes 1572872 | tf_op jit(solution)/shard_map/ppermute | solution.py:85
  16.6 40.2 %collective-permute-start.2 = (bf16[256,1024]{1,0:T(8,128)(2,1)S(1)}, bf16[256,1024]{1,0:T(8,128)(2,1)S(1)}, u32[]{:S(2)}, u32[]{:S(2)}) collective-permute-start(bf16[256,1024]{1,0:T(8,128)(2,1)S(1)} %get-tuple-element.46), channel_id=1, source_target_pairs={{0,130},{4,134},{8,138},{12,142},{16,146},{20,150},{24,154},{28,15... | collective-permute-start | bytes 1572872 | tf_op jit(solution)/shard_map/ppermute | solution.py:85
  27.5 60.6 %copy-start = (bf16[768,512]{1,0:T(8,128)(2,1)}, bf16[768,512]{1,0:T(8,128)(2,1)S(1)}, u32[]{:S(2)}) copy-start(bf16[768,512]{1,0:T(8,128)(2,1)S(1)} %collective-permute-done.3.refs_1_) | copy-start | bytes 2359300
  27.5 29.2 %collective-permute-start.4 = (bf16[384,512]{1,0:T(8,128)(2,1)S(1)}, bf16[384,512]{1,0:T(8,128)(2,1)S(1)}, u32[]{:S(2)}, u32[]{:S(2)}) collective-permute-start(bf16[384,512]{1,0:T(8,128)(2,1)S(1)} %slice.48), channel_id=1, source_target_pairs={{0,4},{1,5},{2,6},{3,7},{4,8},{5,9},{6,10},{7,11},{8,12},{9,13},{1... | collective-permute-start | bytes 1179656 | tf_op jit(solution)/shard_map/ppermute | solution.py:76
  29.1 100.9 %copy-start.1 = (bf16[768,512]{1,0:T(8,128)(2,1)}, bf16[768,512]{1,0:T(8,128)(2,1)S(1)}, u32[]{:S(2)}) copy-start(bf16[768,512]{1,0:T(8,128)(2,1)S(1)} %collective-permute-done.5.refs_4_) | copy-start | bytes 2359300
  29.1 27.6 %collective-permute-start.6 = (bf16[384,512]{1,0:T(8,128)(2,1)S(1)}, bf16[384,512]{1,0:T(8,128)(2,1)S(1)}, u32[]{:S(2)}, u32[]{:S(2)}) collective-permute-start(bf16[384,512]{1,0:T(8,128)(2,1)S(1)} %slice.49), channel_id=1, source_target_pairs={{0,12},{1,13},{2,14},{3,15},{4,0},{5,1},{6,2},{7,3},{8,4},{9,5},{1... | collective-permute-start | bytes 1179656 | tf_op jit(solution)/shard_map/ppermute | solution.py:76
  56.7 27.2 %copy-start.6 = (bf16[768,512]{1,0:T(8,128)(2,1)}, bf16[768,512]{1,0:T(8,128)(2,1)S(1)}, u32[]{:S(2)}) copy-start(bf16[768,512]{1,0:T(8,128)(2,1)S(1)} %collective-permute-done.refs_5_) | copy-start | bytes 2359300
  56.8 27.2 %copy-start.8 = (bf16[384,512]{1,0:T(8,128)(2,1)}, bf16[384,512]{1,0:T(8,128)(2,1)S(1)}, u32[]{:S(2)}) copy-start(bf16[384,512]{1,0:T(8,128)(2,1)S(1)} %collective-permute-done.4.refs_2_) | copy-start | bytes 1179652
  56.8 27.2 %copy-start.9 = (bf16[384,512]{1,0:T(8,128)(2,1)}, bf16[384,512]{1,0:T(8,128)(2,1)S(1)}, u32[]{:S(2)}) copy-start(bf16[384,512]{1,0:T(8,128)(2,1)S(1)} %collective-permute-done.6.refs_3_) | copy-start | bytes 1179652
  56.8 27.2 %collective-permute-start.9 = (bf16[768,512]{1,0:T(8,128)(2,1)S(1)}, bf16[768,512]{1,0:T(8,128)(2,1)S(1)}, u32[]{:S(2)}, u32[]{:S(2)}) collective-permute-start(bf16[768,512]{1,0:T(8,128)(2,1)S(1)} %collective-permute-done.refs_5_), channel_id=1, source_target_pairs={{0,4},{1,5},{2,6},{3,7},{4,8},{5,9},{6,10},{7,11},{8,12},{9,13},{1... | collective-permute-start | bytes 2359304 | tf_op jit(solution)/shard_map/ppermute | solution.py:76
  58.4 25.6 %collective-permute-start.10 = (bf16[768,512]{1,0:T(8,128)(2,1)S(1)}, bf16[768,512]{1,0:T(8,128)(2,1)S(1)}, u32[]{:S(2)}, u32[]{:S(2)}) collective-permute-start(bf16[768,512]{1,0:T(8,128)(2,1)S(1)} %collective-permute-done.refs_5_), channel_id=1, source_target_pairs={{0,12},{1,13},{2,14},{3,15},{4,0},{5,1},{6,2},{7,3},{8,4},{9,5},{1... | collective-permute-start | bytes 2359304 | tf_op jit(solution)/shard_map/ppermute | solution.py:76
  58.9 25.1 %collective-permute-start.7 = (bf16[256,1024]{1,0:T(8,128)(2,1)S(1)}, bf16[256,1024]{1,0:T(8,128)(2,1)S(1)}, u32[]{:S(2)}, u32[]{:S(2)}) collective-permute-start(bf16[256,1024]{1,0:T(8,128)(2,1)S(1)} %collective-permute-done.1), channel_id=1, source_target_pairs={{0,2},{4,6},{8,10},{12,14},{16,18},{20,22},{24,26},{28,30},{32,34}... | collective-permute-start | bytes 1572872 | tf_op jit(solution)/shard_map/ppermute | solution.py:85
  58.9 25.1 %collective-permute-start.8 = (bf16[256,1024]{1,0:T(8,128)(2,1)S(1)}, bf16[256,1024]{1,0:T(8,128)(2,1)S(1)}, u32[]{:S(2)}, u32[]{:S(2)}) collective-permute-start(bf16[256,1024]{1,0:T(8,128)(2,1)S(1)} %collective-permute-done.2), channel_id=1, source_target_pairs={{0,130},{4,134},{8,138},{12,142},{16,146},{20,150},{24,154},{28,15... | collective-permute-start | bytes 1572872 | tf_op jit(solution)/shard_map/ppermute | solution.py:85
  84.0 48.3 %copy-start.2 = (bf16[768,512]{1,0:T(8,128)(2,1)}, bf16[768,512]{1,0:T(8,128)(2,1)S(1)}, u32[]{:S(2)}) copy-start(bf16[768,512]{1,0:T(8,128)(2,1)S(1)} %collective-permute-done.9.refs_6_) | copy-start | bytes 2359300
  84.0 48.2 %copy-start.3 = (bf16[768,512]{1,0:T(8,128)(2,1)}, bf16[768,512]{1,0:T(8,128)(2,1)S(1)}, u32[]{:S(2)}) copy-start(bf16[768,512]{1,0:T(8,128)(2,1)S(1)} %collective-permute-done.10.refs_9_) | copy-start | bytes 2359300
  85.2 21.4 %collective-permute-start.13 = (bf16[768,512]{1,0:T(8,128)(2,1)}, bf16[768,512]{1,0:T(8,128)(2,1)S(1)}, u32[]{:S(2)}, u32[]{:S(2)}) collective-permute-start(bf16[768,512]{1,0:T(8,128)(2,1)} %copy-done.6), channel_id=1, source_target_pairs={{0,1},{1,2},{2,3},{3,0},{4,5},{5,6},{6,7},{7,4},{8,9},{9,10},{10,1... | collective-permute-start | bytes 2359304 | tf_op jit(solution)/shard_map/ppermute | solution.py:79
  86.6 11.3 %collective-permute-start.11 = (bf16[384,512]{1,0:T(8,128)(2,1)S(1)}, bf16[384,512]{1,0:T(8,128)(2,1)S(1)}, u32[]{:S(2)}, u32[]{:S(2)}) collective-permute-start(bf16[384,512]{1,0:T(8,128)(2,1)S(1)} %slice.40), channel_id=1, source_target_pairs={{0,4},{1,5},{2,6},{3,7},{4,8},{5,9},{6,10},{7,11},{8,12},{9,13},{1... | collective-permute-start | bytes 1179656 | tf_op jit(solution)/shard_map/ppermute | solution.py:76
  88.1 9.9 %collective-permute-start.12 = (bf16[384,512]{1,0:T(8,128)(2,1)S(1)}, bf16[384,512]{1,0:T(8,128)(2,1)S(1)}, u32[]{:S(2)}, u32[]{:S(2)}) collective-permute-start(bf16[384,512]{1,0:T(8,128)(2,1)S(1)} %slice.41), channel_id=1, source_target_pairs={{0,12},{1,13},{2,14},{3,15},{4,0},{5,1},{6,2},{7,3},{8,4},{9,5},{1... | collective-permute-start | bytes 1179656 | tf_op jit(solution)/shard_map/ppermute | solution.py:76
  97.9 35.3 %copy-start.10 = (bf16[384,512]{1,0:T(8,128)(2,1)}, bf16[384,512]{1,0:T(8,128)(2,1)S(1)}, u32[]{:S(2)}) copy-start(bf16[384,512]{1,0:T(8,128)(2,1)S(1)} %collective-permute-done.11.refs_7_) | copy-start | bytes 1179652
  98.1 31.1 %copy-start.11 = (bf16[384,512]{1,0:T(8,128)(2,1)}, bf16[384,512]{1,0:T(8,128)(2,1)S(1)}, u32[]{:S(2)}) copy-start(bf16[384,512]{1,0:T(8,128)(2,1)S(1)} %collective-permute-done.12.refs_8_) | copy-start | bytes 1179652
  106.6 26.6 %copy-start.7 = (bf16[768,512]{1,0:T(8,128)(2,1)}, bf16[768,512]{1,0:T(8,128)(2,1)S(1)}, u32[]{:S(2)}) copy-start(bf16[768,512]{1,0:T(8,128)(2,1)S(1)} %collective-permute-done.13.refs_2_) | copy-start | bytes 2359300
  106.6 19.5 %collective-permute-start.14 = (bf16[768,512]{1,0:T(8,128)(2,1)S(1)}, bf16[768,512]{1,0:T(8,128)(2,1)S(1)}, u32[]{:S(2)}, u32[]{:S(2)}) collective-permute-start(bf16[768,512]{1,0:T(8,128)(2,1)S(1)} %collective-permute-done.13.refs_2_), channel_id=1, source_target_pairs={{0,4},{1,5},{2,6},{3,7},{4,8},{5,9},{6,10},{7,11},{8,12},{9,13},{1... | collective-permute-start | bytes 2359304 | tf_op jit(solution)/shard_map/ppermute | solution.py:76
  108.0 20.0 %collective-permute-start.15 = (bf16[768,512]{1,0:T(8,128)(2,1)S(1)}, bf16[768,512]{1,0:T(8,128)(2,1)}, u32[]{:S(2)}, u32[]{:S(2)}) collective-permute-start(bf16[768,512]{1,0:T(8,128)(2,1)S(1)} %collective-permute-done.13.refs_2_), channel_id=1, source_target_pairs={{0,1},{1,2},{2,3},{3,0},{4,5},{5,6},{6,7},{7,4},{8,9},{9,10},{10,1... | collective-permute-start | bytes 2359304 | tf_op jit(solution)/shard_map/ppermute | solution.py:79
  108.0 20.0 %collective-permute-start.16 = (bf16[768,512]{1,0:T(8,128)(2,1)S(1)}, bf16[768,512]{1,0:T(8,128)(2,1)S(1)}, u32[]{:S(2)}, u32[]{:S(2)}) collective-permute-start(bf16[768,512]{1,0:T(8,128)(2,1)S(1)} %collective-permute-done.13.refs_2_), channel_id=1, source_target_pairs={{0,12},{1,13},{2,14},{3,15},{4,0},{5,1},{6,2},{7,3},{8,4},{9,5},{1... | collective-permute-start | bytes 2359304 | tf_op jit(solution)/shard_map/ppermute | solution.py:76
  126.1 23.8 %copy-start.4 = (bf16[768,512]{1,0:T(8,128)(2,1)}, bf16[768,512]{1,0:T(8,128)(2,1)S(1)}, u32[]{:S(2)}) copy-start(bf16[768,512]{1,0:T(8,128)(2,1)S(1)} %collective-permute-done.14.refs_3_) | copy-start | bytes 2359300
  128.0 5.3 %copy-start.5 = (bf16[768,512]{1,0:T(8,128)(2,1)}, bf16[768,512]{1,0:T(8,128)(2,1)S(1)}, u32[]{:S(2)}) copy-start(bf16[768,512]{1,0:T(8,128)(2,1)S(1)} %collective-permute-done.16.refs_6_) | copy-start | bytes 2359300
  128.0 27.9 %collective-permute-start.19 = (bf16[768,512]{1,0:T(8,128)(2,1)}, bf16[768,512]{1,0:T(8,128)(2,1)}, u32[]{:S(2)}, u32[]{:S(2)}) collective-permute-start(bf16[768,512]{1,0:T(8,128)(2,1)} %collective-permute-done.15.refs_7_), channel_id=1, source_target_pairs={{0,4},{1,5},{2,6},{3,7},{4,8},{5,9},{6,10},{7,11},{8,12},{9,13},{1... | collective-permute-start | bytes 2359304 | tf_op jit(solution)/shard_map/ppermute | solution.py:76
  129.2 26.7 %collective-permute-start.20 = (bf16[768,512]{1,0:T(8,128)(2,1)}, bf16[768,512]{1,0:T(8,128)(2,1)}, u32[]{:S(2)}, u32[]{:S(2)}) collective-permute-start(bf16[768,512]{1,0:T(8,128)(2,1)} %collective-permute-done.15.refs_7_), channel_id=1, source_target_pairs={{0,12},{1,13},{2,14},{3,15},{4,0},{5,1},{6,2},{7,3},{8,4},{9,5},{1... | collective-permute-start | bytes 2359304 | tf_op jit(solution)/shard_map/ppermute | solution.py:76
  130.1 24.1 %collective-permute-start.17 = (bf16[384,512]{1,0:T(8,128)(2,1)S(1)}, bf16[384,512]{1,0:T(8,128)(2,1)}, u32[]{:S(2)}, u32[]{:S(2)}) collective-permute-start(bf16[384,512]{1,0:T(8,128)(2,1)S(1)} %slice.42), channel_id=1, source_target_pairs={{0,4},{1,5},{2,6},{3,7},{4,8},{5,9},{6,10},{7,11},{8,12},{9,13},{1... | collective-permute-start | bytes 1179656 | tf_op jit(solution)/shard_map/ppermute | solution.py:76
  132.3 23.6 %collective-permute-start.18 = (bf16[384,512]{1,0:T(8,128)(2,1)S(1)}, bf16[384,512]{1,0:T(8,128)(2,1)S(1)}, u32[]{:S(2)}, u32[]{:S(2)}) collective-permute-start(bf16[384,512]{1,0:T(8,128)(2,1)S(1)} %slice.43), channel_id=1, source_target_pairs={{0,12},{1,13},{2,14},{3,15},{4,0},{5,1},{6,2},{7,3},{8,4},{9,5},{1... | collective-permute-start | bytes 1179656 | tf_op jit(solution)/shard_map/ppermute | solution.py:76
  137.2 23.1 %copy-start.16 = (s32[192]{0:T(256)S(1)}, s32[192]{0:T(256)}, u32[]{:S(2)}) copy-start(s32[192]{0:T(256)} %param.9) | copy-start | bytes 2308
  155.9 5.2 %copy-start.12 = (bf16[384,512]{1,0:T(8,128)(2,1)}, bf16[384,512]{1,0:T(8,128)(2,1)S(1)}, u32[]{:S(2)}) copy-start(bf16[384,512]{1,0:T(8,128)(2,1)S(1)} %collective-permute-done.18.refs_5_) | copy-start | bytes 1179652
  157.0 18.7 %collective-permute-start.21 = (bf16[384,512]{1,0:T(8,128)(2,1)S(1)}, bf16[384,512]{1,0:T(8,128)(2,1)S(1)}, u32[]{:S(2)}, u32[]{:S(2)}) collective-permute-start(bf16[384,512]{1,0:T(8,128)(2,1)S(1)} %slice.44), channel_id=1, source_target_pairs={{0,4},{1,5},{2,6},{3,7},{4,8},{5,9},{6,10},{7,11},{8,12},{9,13},{1... | collective-permute-start | bytes 1179656 | tf_op jit(solution)/shard_map/ppermute | solution.py:76
  159.9 15.9 %collective-permute-start.22 = (bf16[384,512]{1,0:T(8,128)(2,1)S(1)}, bf16[384,512]{1,0:T(8,128)(2,1)S(1)}, u32[]{:S(2)}, u32[]{:S(2)}) collective-permute-start(bf16[384,512]{1,0:T(8,128)(2,1)S(1)} %slice.45), channel_id=1, source_target_pairs={{0,12},{1,13},{2,14},{3,15},{4,0},{5,1},{6,2},{7,3},{8,4},{9,5},{1... | collective-permute-start | bytes 1179656 | tf_op jit(solution)/shard_map/ppermute | solution.py:76
  175.8 0.7 copy-start.13
  175.8 0.9 copy-start.14
  184.0 4.1 %collective-permute-start.23 = (f32[8,768]{1,0:T(8,128)}, f32[8,768]{1,0:T(8,128)S(1)}, u32[]{:S(2)}, u32[]{:S(2)}) collective-permute-start(f32[8,768]{1,0:T(8,128)} %get-tuple-element.42.own_ref), channel_id=1, source_target_pairs={{0,1},{1,0},{2,3},{3,2},{4,5},{5,4},{6,7},{7,6},{8,9},{9,8},{10,11... | collective-permute-start | bytes 73736 | tf_op jit(solution)/shard_map/ppermute | solution.py:334
  188.2 0.6 copy-start.15
  190.8 4.7 %collective-permute-start.24 = (f32[1,128]{1,0:T(1,128)}, f32[1,128]{1,0:T(1,128)S(1)}, u32[]{:S(2)}, u32[]{:S(2)}) collective-permute-start(f32[1,128]{1,0:T(1,128)} %get-tuple-element.45), channel_id=1, source_target_pairs={{0,2},{1,3},{2,0},{3,1},{4,6},{5,7},{6,4},{7,5},{8,10},{9,11},{10,... | collective-permute-start | bytes 1544 | tf_op jit(solution)/shard_map/ppermute | solution.py:323
  196.1 6.9 %collective-permute-start.27 = (f32[1,128]{1,0:T(1,128)S(1)}, f32[1,128]{1,0:T(1,128)S(1)}, u32[]{:S(2)}, u32[]{:S(2)}) collective-permute-start(f32[1,128]{1,0:T(1,128)S(1)} %add.337), channel_id=1, source_target_pairs={{0,144},{16,128},{32,176},{48,160},{64,208},{80,192},{96,240},{112... | collective-permute-start | bytes 1544 | tf_op jit(solution)/shard_map/ppermute | solution.py:323
  196.1 7.5 %collective-permute-start.26 = (f32[1,128]{1,0:T(1,128)S(1)}, f32[1,128]{1,0:T(1,128)S(1)}, u32[]{:S(2)}, u32[]{:S(2)}) collective-permute-start(f32[1,128]{1,0:T(1,128)S(1)} %add.337), channel_id=1, source_target_pairs={{0,128},{16,144},{32,160},{48,176},{64,192},{80,208},{96,224},{112... | collective-permute-start | bytes 1544 | tf_op jit(solution)/shard_map/ppermute | solution.py:323
  196.2 7.4 %collective-permute-start.25 = (f32[1,128]{1,0:T(1,128)S(1)}, f32[1,128]{1,0:T(1,128)S(1)}, u32[]{:S(2)}, u32[]{:S(2)}) collective-permute-start(f32[1,128]{1,0:T(1,128)S(1)} %add.337), channel_id=1, source_target_pairs={{0,16},{16,0},{32,48},{48,32},{64,80},{80,64},{96,112},{112,96},{1... | collective-permute-start | bytes 1544 | tf_op jit(solution)/shard_map/ppermute | solution.py:323
  203.6 4.6 %collective-permute-start.30 = (f32[1,128]{1,0:T(1,128)S(1)}, f32[1,128]{1,0:T(1,128)S(1)}, u32[]{:S(2)}, u32[]{:S(2)}) collective-permute-start(f32[1,128]{1,0:T(1,128)S(1)} %add_add_fusion.2), channel_id=1, source_target_pairs={{0,96},{16,112},{32,0},{48,16},{64,32},{80,48},{96,64},{112,80},{1... | collective-permute-start | bytes 1544 | tf_op jit(solution)/shard_map/ppermute | solution.py:323
  206.7 5.0 %collective-permute-start.29 = (f32[1,128]{1,0:T(1,128)S(1)}, f32[1,128]{1,0:T(1,128)S(1)}, u32[]{:S(2)}, u32[]{:S(2)}) collective-permute-start(f32[1,128]{1,0:T(1,128)S(1)} %add_add_fusion.2), channel_id=1, source_target_pairs={{0,64},{16,80},{32,96},{48,112},{64,0},{80,16},{96,32},{112,48},{1... | collective-permute-start | bytes 1544 | tf_op jit(solution)/shard_map/ppermute | solution.py:323
  207.3 4.8 %collective-permute-start.28 = (f32[1,128]{1,0:T(1,128)S(1)}, f32[1,128]{1,0:T(1,128)S(1)}, u32[]{:S(2)}, u32[]{:S(2)}) collective-permute-start(f32[1,128]{1,0:T(1,128)S(1)} %add_add_fusion.2), channel_id=1, source_target_pairs={{0,32},{16,48},{32,64},{48,80},{64,96},{80,112},{96,0},{112,16},{1... | collective-permute-start | bytes 1544 | tf_op jit(solution)/shard_map/ppermute | solution.py:323
  212.0 10.9 %collective-permute-start.33 = (f32[1,128]{1,0:T(1,128)S(1)}, f32[1,128]{1,0:T(1,128)S(1)}, u32[]{:S(2)}, u32[]{:S(2)}) collective-permute-start(f32[1,128]{1,0:T(1,128)S(1)} %add_add_fusion.1), channel_id=1, source_target_pairs={{0,12},{1,13},{2,14},{3,15},{4,0},{5,1},{6,2},{7,3},{8,4},{9,5},{1... | collective-permute-start | bytes 1544 | tf_op jit(solution)/shard_map/ppermute | solution.py:323
  214.8 8.1 %collective-permute-start.32 = (f32[1,128]{1,0:T(1,128)S(1)}, f32[1,128]{1,0:T(1,128)S(1)}, u32[]{:S(2)}, u32[]{:S(2)}) collective-permute-start(f32[1,128]{1,0:T(1,128)S(1)} %add_add_fusion.1), channel_id=1, source_target_pairs={{0,8},{1,9},{2,10},{3,11},{4,12},{5,13},{6,14},{7,15},{8,0},{9,1},... | collective-permute-start | bytes 1544 | tf_op jit(solution)/shard_map/ppermute | solution.py:323
  215.3 7.6 %collective-permute-start.31 = (f32[1,128]{1,0:T(1,128)S(1)}, f32[1,128]{1,0:T(1,128)S(1)}, u32[]{:S(2)}, u32[]{:S(2)}) collective-permute-start(f32[1,128]{1,0:T(1,128)S(1)} %add_add_fusion.1), channel_id=1, source_target_pairs={{0,4},{1,5},{2,6},{3,7},{4,8},{5,9},{6,10},{7,11},{8,12},{9,13},{1... | collective-permute-start | bytes 1544 | tf_op jit(solution)/shard_map/ppermute | solution.py:323
Sparse Core Ops, SparseCore 0:
  9.9 55.2 all-gather.4
  85.3 51.8 all-gather.6
